TPU v7x, 32 devices: a whole 2x2x4 slice. The times are simulated.
32 devices in a mesh: seq: 8 (over y, x, core), grp: 4 (over z).
Axes of the slice: x: 2, y: 2, z: 4, core: 2. Of those that a mesh axis runs over, the one named last changes fastest.
Arguments:
- tokens: bfloat16 [4, 2048, 1024], P('grp', 'seq'), may hold values from -6 to 6
- memory: bfloat16 [4, 320, 1024], P('grp', 'seq'), may hold values from -6 to 6
- cotangent: bfloat16 [4, 2048, 1024], P('grp', 'seq'), may hold values from -6 to 6
- windows: int32 [4], P('grp'), may hold values from 512 to 2048, as said below
- mem_lengths: int32 [4], P('grp'), may hold values from 60 to 320, as said below
- owners: int32 [64], replicated, may hold values from 0 to 31, as said below
- master: float32 [96, 256, 1024], P(('seq', 'grp'))
- first_moment: float32 [96, 256, 1024], P(('seq', 'grp'))
- second_moment: float32 [96, 256, 1024], P(('seq', 'grp')), as said below
- vectors: float32 [17, 1024], replicated
- vec_first: float32 [17, 1024], replicated, may hold values from -256 to 256
- vec_second: float32 [17, 1024], replicated, may hold values from 682.6667 to 2730.6667
Outputs:
- mixed: bfloat16 [4, 2048, 1024], P('grp', 'seq')
- grad_tokens: float32 [4, 2048, 1024], P('grp', 'seq')
- grad_memory: float32 [4, 320, 1024], P('grp', 'seq')
- new_first: float32 [96, 256, 1024], P(('seq', 'grp'))
- new_second: float32 [96, 256, 1024], P(('seq', 'grp'))
- new_master: float32 [96, 256, 1024], P(('seq', 'grp'))
- master_copy: bfloat16 [96, 256, 1024], P(('seq', 'grp'))
- vec_first_out: float32 [17, 1024], replicated
- vec_second_out: float32 [17, 1024], replicated
- vectors_out: float32 [17, 1024], replicated
- grad_out_bias: float32 [1024], replicated
Inputs may be any that keep to these rules, and one draw needn't show every extreme that they name: `owners`: each device owns at most 3 units and half of the devices own exactly 3. `windows`: one sequence of each group of 1 sequence has window 2048. `mem_lengths`: one sequence of each group of 1 sequence has all 320 memory keys valid; valid keys come first. `second_moment`: positive.
All inputs are finite; a program needn't handle non-finite values.
Results may differ from a plain program's by a relative error of at most 0.024.
Values may be sent and summed in bfloat16 or wider, within the bound.
A program may use at most 448 MiB of HBM per device.

v0:
```python
import jax
import jax.numpy as jnp
from jax import lax
from jax.sharding import PartitionSpec as P

D = 1024
FF = 4096
HEADS = 16
HDIM = 64
STEP = 10


NEG_FILL = -1e30
NORM_EPS = 1e-05
BETA_ONE = 0.5
BETA_TWO = 0.75
RATE_MATRIX = 0.03
RATE_VECTOR = 0.4
WEIGHT_DECAY = 0.01
ADAM_EPS = 1e-08


def passed_along(block, axis, distance):
    devices = range(lax.axis_size(axis))
    route = [(i - distance, i) for i in devices if i - distance in devices]
    return lax.ppermute(block, axis, route)


def shifted(block, axis, distance):
    devices = range(lax.axis_size(axis))
    route = [((i - distance) % len(devices), i) for i in devices]
    return lax.ppermute(block, axis, route)


def product(left, right):
    return jnp.dot(left, right, preferred_element_type=jnp.float32)


def product_tn(left, right):
    return jnp.einsum("rd,re->de", left, right, preferred_element_type=jnp.float32)


def product_nt(left, right):
    return jnp.einsum("rd,ed->re", left, right, preferred_element_type=jnp.float32)


def slot_tables(owners, slot_count, holders):
    unit_count = owners.shape[0]
    positions = lax.iota(jnp.int32, unit_count)
    same_owner = owners[None, :] == owners[:, None]
    slot_rank = jnp.sum(
        (same_owner & (positions[None, :] < positions[:, None])).astype(jnp.int32), axis=1
    )
    placed = owners * slot_count + slot_rank
    slot_ids = lax.iota(jnp.int32, holders * slot_count)
    matches = slot_ids[:, None] == placed[None, :]
    occupied = jnp.sum(matches.astype(jnp.int32), axis=1) > 0
    unit_at = jnp.sum(jnp.where(matches, positions[None, :], 0), axis=1)
    return (placed, unit_at, occupied)


def norm_forward(stream, gain_row, shift_row):
    row_mean = jnp.mean(stream, axis=-1, keepdims=True)
    centered = stream - row_mean
    inverse = lax.rsqrt(jnp.mean(centered * centered, axis=-1, keepdims=True) + NORM_EPS)
    normal_form = centered * inverse
    return (normal_form * gain_row + shift_row, normal_form, inverse)


def norm_backward(upstream, normal_form, inverse, gain_row):
    scaled = upstream * gain_row
    first_term = jnp.mean(scaled, axis=-1, keepdims=True)
    second_term = jnp.mean(scaled * normal_form, axis=-1, keepdims=True)
    grad_in = inverse * (scaled - first_term - normal_form * second_term)
    return (grad_in, jnp.sum(upstream * normal_form, axis=0), jnp.sum(upstream, axis=0))


def gelu_exact(values):
    return jax.nn.gelu(values, approximate=False)


def head_view(tensor):
    return tensor.reshape(tensor.shape[0], tensor.shape[1], HEADS, HDIM)


def joined_heads(tensor):
    return tensor.reshape(tensor.shape[0], tensor.shape[1], HEADS * HDIM)


def causal_mask(query_pos, key_pos, windows):
    earlier = key_pos[None, None, :] <= query_pos[None, :, None]
    inside = key_pos[None, None, :] > query_pos[None, :, None] - windows[:, None, None]
    return (earlier & inside)[:, None]


def tile_probs(query_rows, key_rows, allowed):
    scores = HDIM ** (-0.5) * jnp.einsum(
        "sqhd,skhd->shqk",
        head_view(query_rows),
        head_view(key_rows),
        preferred_element_type=jnp.float32,
    )
    masked = jnp.where(allowed, scores, NEG_FILL)
    block_top = jnp.max(masked, axis=-1)
    prob_tile = jnp.where(allowed, jnp.exp(masked - block_top[..., None]), 0.0)
    return (prob_tile, block_top)


def tile_grads(
    query_rows, key_rows, value_rows, grad_rows, row_best, row_total, row_delta, allowed
):
    prob_tile, block_top = tile_probs(query_rows, key_rows, allowed)
    lifted = jnp.exp(block_top - row_best) / row_total
    grad_heads = jnp.swapaxes(head_view(grad_rows).astype(jnp.float32), 1, 2)
    grad_parts = (grad_heads * lifted[..., None]).astype(jnp.bfloat16)
    grad_probs = jnp.einsum(
        "shqd,skhd->shqk", grad_parts, head_view(value_rows), preferred_element_type=jnp.float32
    )
    grad_scores = (prob_tile * (grad_probs - (lifted * row_delta)[..., None])).astype(jnp.bfloat16)
    return (prob_tile.astype(jnp.bfloat16), grad_parts, grad_scores)


def tile_query_grad(grad_scores, key_rows):
    return HDIM ** (-0.5) * jnp.einsum(
        "shqk,skhd->sqhd", grad_scores, head_view(key_rows), preferred_element_type=jnp.float32
    )


def tile_key_grads(prob_bf, grad_parts, grad_scores, query_rows):
    key_part = HDIM ** (-0.5) * jnp.einsum(
        "shqk,sqhd->skhd", grad_scores, head_view(query_rows), preferred_element_type=jnp.float32
    )
    value_part = jnp.einsum(
        "shqk,shqd->skhd", prob_bf, grad_parts, preferred_element_type=jnp.float32
    )
    return (joined_heads(key_part), joined_heads(value_part))


def split_blocks(piece, block_rows):
    block_count = piece.shape[1] // block_rows
    return jnp.swapaxes(
        piece.reshape(piece.shape[0], block_count, block_rows, piece.shape[2]), 0, 1
    )


def adam_step(weight, first, second_in, upstream, rate, decay):
    first_new = BETA_ONE * first + (1.0 - BETA_ONE) * upstream
    second_new = BETA_TWO * second_in + (1.0 - BETA_TWO) * upstream * upstream
    first_hat = first_new / (1.0 - BETA_ONE**STEP)
    second_hat = second_new / (1.0 - BETA_TWO**STEP)
    weight_new = weight - rate * (first_hat / (jnp.sqrt(second_hat) + ADAM_EPS) + decay * weight)
    return (first_new, second_new, weight_new)


def local(
    tokens,
    memory,
    cotangent,
    windows,
    mem_lengths,
    owners,
    master,
    first_moment,
    second_moment,
    vectors,
    vec_first,
    vec_second,
):
    seq_count, block_rows, width = tokens.shape
    flat_rows = seq_count * block_rows
    cycle_size = lax.axis_size("seq")
    holders = lax.axis_size("seq") * lax.axis_size("grp")
    slot_count, unit_rows = (master.shape[0], master.shape[1])
    bias_rows = FF // D
    placed, unit_at, occupied = slot_tables(owners, slot_count, holders)
    gathered = lax.all_gather(master.astype(jnp.bfloat16), ("seq", "grp"), axis=0, tiled=True)
    stacked = jnp.take(gathered, placed, axis=0).reshape(-1, D)
    self_query = stacked[0:D]
    self_key = stacked[D : 2 * D]
    self_value = stacked[2 * D : 3 * D]
    self_out = stacked[3 * D : 4 * D]
    cross_query = stacked[4 * D : 5 * D]
    cross_key = stacked[5 * D : 6 * D]
    cross_value = stacked[6 * D : 7 * D]
    cross_out = stacked[7 * D : 8 * D]
    hidden_in = stacked[8 * D : 8 * D + FF]
    hidden_out = stacked[8 * D + FF :]
    stream = tokens.astype(jnp.float32).reshape(flat_rows, D)
    cycle_index = lax.axis_index("seq")
    query_pos = cycle_index * block_rows + lax.iota(jnp.int32, block_rows)
    normed_one, form_one, inverse_one = norm_forward(stream, vectors[0], vectors[1])
    normed_self = normed_one.astype(jnp.bfloat16)
    query_act = (
        (product(normed_self, self_query) + vectors[6])
        .astype(jnp.bfloat16)
        .reshape(seq_count, block_rows, D)
    )
    key_act = product(normed_self, self_key).astype(jnp.bfloat16).reshape(seq_count, block_rows, D)
    value_act = (
        (product(normed_self, self_value) + vectors[7])
        .astype(jnp.bfloat16)
        .reshape(seq_count, block_rows, D)
    )
    stat_shape = (seq_count, HEADS, block_rows)
    start_state = (
        jnp.full(stat_shape, NEG_FILL, jnp.float32),
        jnp.zeros(stat_shape, jnp.float32),
        jnp.zeros(stat_shape + (HDIM,), jnp.float32),
    )
    key_blocks = split_blocks(lax.all_gather(key_act, "seq", axis=1, tiled=True), block_rows)
    value_blocks = split_blocks(lax.all_gather(value_act, "seq", axis=1, tiled=True), block_rows)

    def one_block(running, block_item):
        row_best, row_total, accumulated = running
        key_tile, value_tile, block_index = block_item
        key_pos = block_index * block_rows + lax.iota(jnp.int32, block_rows)
        prob_tile, block_top = tile_probs(
            query_act, key_tile, causal_mask(query_pos, key_pos, windows)
        )
        block_part = jnp.einsum(
            "shqk,skhd->shqd",
            prob_tile.astype(jnp.bfloat16),
            head_view(value_tile),
            preferred_element_type=jnp.float32,
        )
        new_best = jnp.maximum(row_best, block_top)
        keep_old = jnp.exp(row_best - new_best)
        keep_new = jnp.exp(block_top - new_best)
        row_total = row_total * keep_old + keep_new * jnp.sum(prob_tile, axis=-1)
        accumulated = accumulated * keep_old[..., None] + keep_new[..., None] * block_part
        return ((new_best, row_total, accumulated), None)

    result, _ = lax.scan(
        one_block, start_state, (key_blocks, value_blocks, lax.iota(jnp.int32, key_blocks.shape[0]))
    )
    row_best, row_total, accumulated = result
    attended32 = accumulated / row_total[..., None]
    attended = (
        joined_heads(jnp.swapaxes(attended32, 1, 2)).astype(jnp.bfloat16).reshape(flat_rows, D)
    )
    after_self = stream + product(attended, self_out) + vectors[8]
    normed_two, form_two, inverse_two = norm_forward(after_self, vectors[2], vectors[3])
    normed_cross = normed_two.astype(jnp.bfloat16)
    cross_queries = (
        (product(normed_cross, cross_query) + vectors[9])
        .astype(jnp.bfloat16)
        .reshape(seq_count, block_rows, D)
    )
    memory_whole = lax.all_gather(memory, "seq", axis=1, tiled=True)
    mem_key_act = product(memory_whole, cross_key).astype(jnp.bfloat16)
    mem_value_act = (product(memory_whole, cross_value) + vectors[10]).astype(jnp.bfloat16)
    mem_count = mem_key_act.shape[1]
    mem_allowed = (lax.iota(jnp.int32, mem_count)[None, :] < mem_lengths[:, None])[:, None, None, :]
    cross_probs, cross_top = tile_probs(cross_queries, mem_key_act, mem_allowed)
    cross_total = jnp.sum(cross_probs, axis=-1)
    cross_part = jnp.einsum(
        "shqk,skhd->shqd",
        cross_probs.astype(jnp.bfloat16),
        head_view(mem_value_act),
        preferred_element_type=jnp.float32,
    )
    crossed32 = cross_part / cross_total[..., None]
    crossed = joined_heads(jnp.swapaxes(crossed32, 1, 2)).astype(jnp.bfloat16).reshape(flat_rows, D)
    after_cross = after_self + product(crossed, cross_out) + vectors[11]
    normed_three, form_three, inverse_three = norm_forward(after_cross, vectors[4], vectors[5])
    normed_mlp = normed_three.astype(jnp.bfloat16)
    pre_act = product_nt(normed_mlp, hidden_in) + vectors[12 : 12 + bias_rows].reshape(FF)
    activation, gelu_pull = jax.vjp(gelu_exact, pre_act)
    activation_bf = activation.astype(jnp.bfloat16)
    result_rows = after_cross + product(activation_bf, hidden_out) + vectors[12 + bias_rows]
    mixed = result_rows.astype(jnp.bfloat16).reshape(seq_count, block_rows, D)
    grad_out_bf = cotangent.reshape(flat_rows, D)
    grad_stream = cotangent.astype(jnp.float32).reshape(flat_rows, D)
    grad_hidden_out = product_tn(activation_bf, grad_out_bf)
    grad_down_bias = jnp.sum(grad_stream, axis=0)
    grad_activation = product_nt(grad_out_bf, hidden_out)
    grad_pre = gelu_pull(grad_activation)[0].astype(jnp.bfloat16)
    grad_hidden_in = product_tn(grad_pre, normed_mlp)
    grad_up_bias = jnp.sum(grad_pre.astype(jnp.float32), axis=0)
    grad_normed_mlp = product(grad_pre, hidden_in)
    back_three, grad_gain_three, grad_shift_three = norm_backward(
        grad_normed_mlp, form_three, inverse_three, vectors[4]
    )
    grad_after_cross = grad_stream + back_three
    grad_cross_branch = grad_after_cross.astype(jnp.bfloat16)
    grad_cross_out = product_tn(crossed, grad_cross_branch)
    grad_cross_out_bias = jnp.sum(grad_cross_branch.astype(jnp.float32), axis=0)
    grad_crossed = (
        product_nt(grad_cross_branch, cross_out)
        .astype(jnp.bfloat16)
        .reshape(seq_count, block_rows, D)
    )
    cross_delta = jnp.sum(
        jnp.swapaxes(head_view(grad_crossed).astype(jnp.float32), 1, 2) * crossed32, axis=-1
    )
    cross_prob_bf, cross_grad_parts, cross_grad_scores = tile_grads(
        cross_queries,
        mem_key_act,
        mem_value_act,
        grad_crossed,
        cross_top,
        cross_total,
        cross_delta,
        mem_allowed,
    )
    grad_cross_queries = (
        joined_heads(tile_query_grad(cross_grad_scores, mem_key_act))
        .astype(jnp.bfloat16)
        .reshape(flat_rows, D)
    )
    part_mem_keys, part_mem_values = tile_key_grads(
        cross_prob_bf, cross_grad_parts, cross_grad_scores, cross_queries
    )
    sum_mem_keys, sum_mem_values = (
        lax.psum_scatter(
            part_mem_keys.astype(jnp.bfloat16), "seq", scatter_dimension=1, tiled=True
        ).astype(jnp.float32),
        lax.psum_scatter(
            part_mem_values.astype(jnp.bfloat16), "seq", scatter_dimension=1, tiled=True
        ).astype(jnp.float32),
    )
    grad_mem_keys = sum_mem_keys.astype(jnp.bfloat16)
    grad_mem_values = sum_mem_values.astype(jnp.bfloat16)
    mem_flat = memory.reshape(-1, D)
    mem_keys_flat = grad_mem_keys.reshape(-1, D)
    mem_values_flat = grad_mem_values.reshape(-1, D)
    grad_cross_key = product_tn(mem_flat, mem_keys_flat)
    grad_cross_value = product_tn(mem_flat, mem_values_flat)
    grad_cross_value_bias = jnp.sum(mem_values_flat.astype(jnp.float32), axis=0)
    grad_memory = (
        product_nt(mem_keys_flat, cross_key) + product_nt(mem_values_flat, cross_value)
    ).reshape(memory.shape)
    grad_cross_query = product_tn(normed_cross, grad_cross_queries)
    grad_cross_query_bias = jnp.sum(grad_cross_queries.astype(jnp.float32), axis=0)
    grad_normed_cross = product_nt(grad_cross_queries, cross_query)
    back_two, grad_gain_two, grad_shift_two = norm_backward(
        grad_normed_cross, form_two, inverse_two, vectors[2]
    )
    grad_after_self = grad_after_cross + back_two
    grad_self_branch = grad_after_self.astype(jnp.bfloat16)
    grad_self_out = product_tn(attended, grad_self_branch)
    grad_self_out_bias = jnp.sum(grad_self_branch.astype(jnp.float32), axis=0)
    grad_attended = (
        product_nt(grad_self_branch, self_out)
        .astype(jnp.bfloat16)
        .reshape(seq_count, block_rows, D)
    )
    row_delta = jnp.sum(
        jnp.swapaxes(head_view(grad_attended).astype(jnp.float32), 1, 2) * attended32, axis=-1
    )
    zero_query = jnp.zeros((seq_count, block_rows, HEADS, HDIM), jnp.float32)
    zero_rows = jnp.zeros((seq_count, block_rows, D), jnp.float32)

    def cycle_turn(turn, carry):
        key_tile, value_tile, grad_query_acc, key_acc, value_acc = carry
        anchor = (cycle_index - turn + cycle_size) % cycle_size
        key_pos = anchor * block_rows + lax.iota(jnp.int32, block_rows)
        prob_bf, grad_parts, grad_scores = tile_grads(
            query_act,
            key_tile,
            value_tile,
            grad_attended,
            row_best,
            row_total,
            row_delta,
            causal_mask(query_pos, key_pos, windows),
        )
        key_part, value_part = tile_key_grads(prob_bf, grad_parts, grad_scores, query_act)
        grad_query_acc = grad_query_acc + tile_query_grad(grad_scores, key_tile)
        key_acc = key_acc + key_part
        value_acc = value_acc + value_part
        key_tile, value_tile = passed_along((key_tile, value_tile), "seq", 1)
        key_acc, value_acc = (
            shifted(key_acc.astype(jnp.bfloat16), "seq", 1).astype(key_acc.dtype),
            shifted(value_acc.astype(jnp.bfloat16), "seq", 1).astype(value_acc.dtype),
        )
        return (key_tile, value_tile, grad_query_acc, key_acc, value_acc)

    cycle_state = (key_act, value_act, zero_query, zero_rows, zero_rows)
    cycle_state = lax.fori_loop(0, cycle_size, cycle_turn, cycle_state)
    grad_query_sum = cycle_state[2]
    grad_key_sum = cycle_state[3]
    grad_value_sum = cycle_state[4]
    grad_queries = joined_heads(grad_query_sum).astype(jnp.bfloat16).reshape(flat_rows, D)
    grad_keys = grad_key_sum.astype(jnp.bfloat16).reshape(flat_rows, D)
    grad_values = grad_value_sum.astype(jnp.bfloat16).reshape(flat_rows, D)
    grad_self_query = product_tn(normed_self, grad_queries)
    grad_self_key = product_tn(normed_self, grad_keys)
    grad_self_value = product_tn(normed_self, grad_values)
    grad_query_bias = jnp.sum(grad_queries.astype(jnp.float32), axis=0)
    grad_value_bias = jnp.sum(grad_values.astype(jnp.float32), axis=0)
    grad_normed_self = (
        product_nt(grad_queries, self_query)
        + product_nt(grad_keys, self_key)
        + product_nt(grad_values, self_value)
    )
    back_one, grad_gain_one, grad_shift_one = norm_backward(
        grad_normed_self, form_one, inverse_one, vectors[0]
    )
    grad_tokens = (grad_after_self + back_one).reshape(seq_count, block_rows, D)
    grad_matrices = jnp.concatenate(
        [
            grad_self_query,
            grad_self_key,
            grad_self_value,
            grad_self_out,
            grad_cross_query,
            grad_cross_key,
            grad_cross_value,
            grad_cross_out,
            grad_hidden_in,
            grad_hidden_out,
        ],
        axis=0,
    )
    grad_units = grad_matrices.reshape(-1, unit_rows, D)
    grad_slots = lax.psum_scatter(
        jnp.where(occupied[:, None, None], jnp.take(grad_units, unit_at, axis=0), 0.0),
        ("seq", "grp"),
        scatter_dimension=0,
        tiled=True,
    )
    small_rows = jnp.stack(
        [
            grad_gain_one,
            grad_shift_one,
            grad_gain_two,
            grad_shift_two,
            grad_gain_three,
            grad_shift_three,
            grad_query_bias,
            grad_value_bias,
            grad_self_out_bias,
            grad_cross_query_bias,
            grad_cross_value_bias,
            grad_cross_out_bias,
        ]
    )
    grad_vectors = jnp.concatenate(
        [small_rows, grad_up_bias.reshape(bias_rows, D), grad_down_bias[None]], axis=0
    )
    grad_vectors = lax.psum(grad_vectors, ("seq", "grp"))
    new_first, new_second, new_master = adam_step(
        master, first_moment, second_moment, grad_slots, RATE_MATRIX, WEIGHT_DECAY
    )
    master_copy = new_master.astype(jnp.bfloat16)
    vec_first_out, vec_second_out, vectors_out = adam_step(
        vectors, vec_first, vec_second, grad_vectors, RATE_VECTOR, 0.0
    )
    grad_out_bias = grad_vectors[grad_vectors.shape[0] - 1]
    return (
        mixed,
        grad_tokens,
        grad_memory,
        new_first,
        new_second,
        new_master,
        master_copy,
        vec_first_out,
        vec_second_out,
        vectors_out,
        grad_out_bias,
    )


def solution(mesh):
    placed = (
        P("grp", "seq", None),
        P("grp", "seq", None),
        P("grp", "seq", None),
        P("grp"),
        P("grp"),
        P(),
        P(("seq", "grp"), None, None),
        P(("seq", "grp"), None, None),
        P(("seq", "grp"), None, None),
        P(),
        P(),
        P(),
    )
    return jax.shard_map(
        local,
        mesh=mesh,
        in_specs=placed,
        out_specs=(
            P("grp", "seq", None),
            P("grp", "seq", None),
            P("grp", "seq", None),
            P(("seq", "grp"), None, None),
            P(("seq", "grp"), None, None),
            P(("seq", "grp"), None, None),
            P(("seq", "grp"), None, None),
            P(),
            P(),
            P(),
            P(),
        ),
        check_vma=False,
    )
```

profile of v0, /device:TPU:0, one launch (start us, length us, event | category | flops | bytes accessed | tf_op | source)
XLA Modules:
  0.0 1938.1 jit_solution(952726282847280608)
XLA Ops:
  7.3 3.3 convert_element_type.349
  12.0 277.8 %all-gather.6.cloned.1.call-done = bf16[96,256,1024]{2,1,0:T(8,128)(2,1)} async-done(((bf16[3,256,1024]{2,1,0:T(8,128)(2,1)}), bf16[96,256,1024]{2,1,0:T(8,128)(2,1)}) %all-gather.6.cloned.1.call-update) | async-done | bytes 50331664 | tf_op jit(solution)/shard_map/all_gather | solution.py:176
  289.8 22.9 %gather_fusion = bf16[64,256,1024]{2,1,0:T(8,128)(2,1)} fusion(bf16[96,256,1024]{2,1,0:T(8,128)(2,1)} %all-gather.6.cloned.1.call-done, s32[1024]{0:T(1024)S(1)} %pad_clamp_fusion.1), kind=kCustom, calls=%fused_computation | custom fusion | bytes 67109120 | tf_op jit(solution)/shard_map/jit(_take)/gather | solution.py:177
  312.7 22.8 %broadcast_select_fusion = bf16[64,256,1024]{2,1,0:T(8,128)(2,1)} fusion(bf16[64,256,1024]{2,1,0:T(8,128)(2,1)} %gather_fusion, pred[64]{0:T(512)(128)(4,1)S(1)} %get-tuple-element.691), kind=kLoop, calls=%fused_computation.64 | loop fusion | flops 16777216 | bytes 67108928 | tf_op jit(solution)/shard_map/jit(_take)/select_n | solution.py:177
  335.5 11.4 fusion.136
  350.0 3.1 convolution_convert_fusion.4
  357.2 11.1 all_gather.15
  380.3 12.0 fusion.135
  392.4 34.4 %all-gather.8.cloned.1.call-done = bf16[2048,1024]{1,0:T(8,128)(2,1)} async-done(((bf16[256,1024]{1,0:T(8,128)(2,1)}), bf16[2048,1024]{1,0:T(8,128)(2,1)}) %all-gather.8.cloned.1.call-update) | async-done | bytes 4194320 | tf_op jit(solution)/shard_map/all_gather | solution.py:210
  426.8 64.5 %while.39 = (s32[]{:T(128)}, f32[1,16,256]{2,1,0:T(8,128)S(1)}, f32[1,16,256]{2,1,0:T(8,128)S(1)}, f32[1,16,256,64]{2,3,1,0:T(8,128)}, s32[8]{0:T(128)S(1)}, /*i...) while((s32[]{:T(128)}, f32[1,16,256]{2,1,0:T(8,128)S(1)}, ...), condition=%wide.region_6.7_spmd.clone, body=%wide.region_3.0_spmd.clone.sunk | while | flops 283345664 | bytes 29415664 | solution.py:233
  507.0 16.6 multiply_convert_fusion.2
  523.6 5.9 convert_reduce_fusion
  529.5 3.2 multiply_reduce_fusion
  539.9 5.3 convolution_convert_fusion
  555.0 279.6 %while.40 = (s32[]{:T(128)}, bf16[1,256,1024]{1,2,0:T(8,128)(2,1)}, bf16[1,256,1024]{1,2,0:T(8,128)(2,1)}, f32[1,256,16,64]{1,3,2,0:T(8,128)}, f32[1,256,1024]{1...) while((s32[]{:T(128)}, bf16[1,256,1024]{1,2,0:T(8,128)(2,1)}, ...), condition=%wide.region_21.22_spmd.clone, body=%wide.region_19.21_spmd.clone.sunk | while | flops 691741440 | bytes 56564292 | solution.py:380
  568.4 3.0 collective-permute-start
  571.4 3.1 collective-permute-start.1
  591.8 7.3 collective-permute-start.2
  606.5 4.2 collective-permute-start.1
  627.1 7.3 collective-permute-start.2
  641.7 5.1 collective-permute-start.1
  663.2 6.4 collective-permute-start.2
  674.2 3.5 collective-permute-start
  677.7 5.3 collective-permute-start.1
  699.4 5.5 collective-permute-start.2
  709.5 4.4 collective-permute-start
  713.9 5.3 collective-permute-start.1
  735.6 4.6 collective-permute-start.2
  744.7 5.3 collective-permute-start
  750.0 5.3 collective-permute-start.1
  771.7 3.7 collective-permute-start.2
  780.0 6.2 collective-permute-start
  786.2 5.3 collective-permute-start.1
  815.3 7.1 collective-permute-start
  822.4 5.3 collective-permute-start.1
  836.1 3.4 fusion.141
  839.6 2.9 convolution_dynamic-update-slice_fusion.7
  842.8 3.9 copy.116
  848.8 2.9 convolution_dynamic-update-slice_fusion.6
  857.3 2.9 convolution_dynamic-update-slice_fusion.3
  866.1 68.8 %all-reduce.8.cloned.1.call-done = (bf16[1,320,1024]{2,0,1:T(2,128)(2,1)}, bf16[1,320,1024]{2,0,1:T(2,128)(2,1)}) async-done(((bf16[1,320,1024]{2,0,1:T(2,128)(2,1)}, bf16[1,320,1024]{2,0,1:T(2,128)(2,1)}), (bf16[1,320,1024]{2,0,1:T(2,128)(2,1)}, bf16[1,320,1024]{2,0,1:T(2,128)(2,1)})) %all-reduce.8.cloned.1.call-update) | async-done | bytes 1310736
  947.6 8.3 convolution_dynamic-update-slice_fusion.1
  955.9 8.1 convolution_dynamic-update-slice_fusion
  964.0 65.6 %gather_fusion.1 = f32[96,256,1024]{2,1,0:T(8,128)} fusion(f32[64,256,1024]{2,1,0:T(8,128)} %bitcast.74, s32[1024]{0:T(1024)} %pad_clamp_fusion), kind=kCustom, calls=%fused_computation.1 | custom fusion | bytes 201326976 | tf_op jit(solution)/shard_map/jit(_take)/gather | solution.py:418
  1029.6 66.4 %select_select_fusion = f32[96,256,1024]{2,1,0:T(8,128)} fusion(f32[96,256,1024]{2,1,0:T(8,128)} %gather_fusion.1, pred[96]{0:T(512)(128)(4,1)S(1)} %copy-done.88, pred[96]{0:T(512)(128)(4,1)S(1)} %copy-done.89), kind=kLoop, calls=%fused_computation.63 | loop fusion | flops 50331648 | bytes 201326784 | tf_op jit(solution)/shard_map/jit(_where)/select_n | solution.py:418
  1100.0 9.3 fusion.73
  1114.6 808.1 %reduce-scatter.2.cloned.1.call-done = f32[3,256,1024]{2,1,0:T(8,128)} async-done(((f32[96,256,1024]{2,1,0:T(8,128)}), f32[3,256,1024]{2,1,0:T(8,128)}) %reduce-scatter.2.cloned.1.call-update) | async-done | bytes 3145744 | tf_op jit(solution)/shard_map/reduce_scatter | solution.py:417
  1922.7 8.4 fusion.131
  (640 shorter events, 322.4 us)
Async XLA Ops:
  7.2 282.6 %all-gather.6.cloned.1.call-start = ((), (), s32[]{:S(2)}) async-start(), calls=%async_computation.1 | async-start | bytes 51904512 | tf_op jit(solution)/shard_map/all_gather | solution.py:176
  10.6 381.8 %all-gather.10.cloned.1.call-start = ((), (), s32[]{:S(2)}) async-start(), calls=%async_computation.5 | async-start | bytes 4718592 | tf_op jit(solution)/shard_map/all_gather | solution.py:211
  11.1 357.9 %copy-start.65 = (f32[256]{0:T(256)}, f32[256]{0:T(256)S(1)}, u32[]{:S(2)}) copy-start(f32[256]{0:T(256)S(1)} %broadcast_multiply_fusion.10) | copy-start | bytes 3076
  11.4 357.6 %copy-start.68 = (f32[256]{0:T(256)}, f32[256]{0:T(256)S(1)}, u32[]{:S(2)}) copy-start(f32[256]{0:T(256)S(1)} %add_rsqrt_fusion.2) | copy-start | bytes 3076
  12.0 356.9 %copy-start.58 = (f32[1,1024]{1,0:T(1,128)}, f32[1,1024]{1,0:T(1,128)S(1)}, u32[]{:S(2)}) copy-start(f32[1,1024]{1,0:T(1,128)S(1)} %get-tuple-element.729) | copy-start | bytes 12292
  12.0 356.9 %copy-start.63 = (f32[1,1024]{1,0:T(1,128)}, f32[1,1024]{1,0:T(1,128)S(1)}, u32[]{:S(2)}) copy-start(f32[1,1024]{1,0:T(1,128)S(1)} %get-tuple-element.728) | copy-start | bytes 12292
  349.9 76.9 %all-gather.8.cloned.1.call-start = ((), (), s32[]{:S(2)}) async-start(), calls=%async_computation.4 | async-start | bytes 4718592 | tf_op jit(solution)/shard_map/all_gather | solution.py:210
  353.1 581.8 %all-reduce.8.cloned.1.call-start = ((), (), s32[]{:S(2)}) async-start(), calls=%async_computation.6 | async-start | bytes 5242880
  564.7 11.2 collective-permute-start.2
  567.1 13.0 collective-permute-start.3
  568.4 13.9 collective-permute-start
  571.4 10.9 collective-permute-start.1
  591.8 21.6 %collective-permute-start.2 = (bf16[1,256,1024]{1,2,0:T(8,128)(2,1)}, bf16[1,256,1024]{1,2,0:T(8,128)(2,1)}, u32[]{:S(2)}, u32[]{:S(2)}) collective-permute-start(bf16[1,256,1024]{1,2,0:T(8,128)(2,1)} %fusion.237), channel_id=1, source_target_pairs={{28,0},{0,4},{4,8},{8,12},{12,16},{16,20},{20,24},{24,28},{29,1},{... | collective-permute-start | bytes 1572872 | tf_op jit(solution)/shard_map/while/body/eval_jaxpr/ppermute | solution.py:32
  601.2 14.3 collective-permute-start.3
  603.7 13.9 collective-permute-start
  606.5 11.1 collective-permute-start.1
  627.1 22.4 %collective-permute-start.2 = (bf16[1,256,1024]{1,2,0:T(8,128)(2,1)}, bf16[1,256,1024]{1,2,0:T(8,128)(2,1)}, u32[]{:S(2)}, u32[]{:S(2)}) collective-permute-start(bf16[1,256,1024]{1,2,0:T(8,128)(2,1)} %fusion.237), channel_id=1, source_target_pairs={{28,0},{0,4},{4,8},{8,12},{12,16},{16,20},{20,24},{24,28},{29,1},{... | collective-permute-start | bytes 1572872 | tf_op jit(solution)/shard_map/while/body/eval_jaxpr/ppermute | solution.py:32
  636.5 15.2 collective-permute-start.3
  638.9 14.8 collective-permute-start
  641.7 12.0 collective-permute-start.1
  663.2 22.5 %collective-permute-start.2 = (bf16[1,256,1024]{1,2,0:T(8,128)(2,1)}, bf16[1,256,1024]{1,2,0:T(8,128)(2,1)}, u32[]{:S(2)}, u32[]{:S(2)}) collective-permute-start(bf16[1,256,1024]{1,2,0:T(8,128)(2,1)} %fusion.237), channel_id=1, source_target_pairs={{28,0},{0,4},{4,8},{8,12},{12,16},{16,20},{20,24},{24,28},{29,1},{... | collective-permute-start | bytes 1572872 | tf_op jit(solution)/shard_map/while/body/eval_jaxpr/ppermute | solution.py:32
  671.7 16.1 collective-permute-start.3
  674.2 15.7 collective-permute-start
  677.7 12.2 collective-permute-start.1
  699.4 22.4 %collective-permute-start.2 = (bf16[1,256,1024]{1,2,0:T(8,128)(2,1)}, bf16[1,256,1024]{1,2,0:T(8,128)(2,1)}, u32[]{:S(2)}, u32[]{:S(2)}) collective-permute-start(bf16[1,256,1024]{1,2,0:T(8,128)(2,1)} %fusion.237), channel_id=1, source_target_pairs={{28,0},{0,4},{4,8},{8,12},{12,16},{16,20},{20,24},{24,28},{29,1},{... | collective-permute-start | bytes 1572872 | tf_op jit(solution)/shard_map/while/body/eval_jaxpr/ppermute | solution.py:32
  707.0 17.0 collective-permute-start.3
  709.5 16.6 collective-permute-start
  713.9 12.2 collective-permute-start.1
  735.6 22.5 %collective-permute-start.2 = (bf16[1,256,1024]{1,2,0:T(8,128)(2,1)}, bf16[1,256,1024]{1,2,0:T(8,128)(2,1)}, u32[]{:S(2)}, u32[]{:S(2)}) collective-permute-start(bf16[1,256,1024]{1,2,0:T(8,128)(2,1)} %fusion.237), channel_id=1, source_target_pairs={{28,0},{0,4},{4,8},{8,12},{12,16},{16,20},{20,24},{24,28},{29,1},{... | collective-permute-start | bytes 1572872 | tf_op jit(solution)/shard_map/while/body/eval_jaxpr/ppermute | solution.py:32
  742.2 17.9 collective-permute-start.3
  744.7 17.5 collective-permute-start
  750.0 12.2 collective-permute-start.1
  771.7 22.4 %collective-permute-start.2 = (bf16[1,256,1024]{1,2,0:T(8,128)(2,1)}, bf16[1,256,1024]{1,2,0:T(8,128)(2,1)}, u32[]{:S(2)}, u32[]{:S(2)}) collective-permute-start(bf16[1,256,1024]{1,2,0:T(8,128)(2,1)} %fusion.237), channel_id=1, source_target_pairs={{28,0},{0,4},{4,8},{8,12},{12,16},{16,20},{20,24},{24,28},{29,1},{... | collective-permute-start | bytes 1572872 | tf_op jit(solution)/shard_map/while/body/eval_jaxpr/ppermute | solution.py:32
  777.5 18.8 collective-permute-start.3
  780.0 18.4 collective-permute-start
  786.2 12.2 collective-permute-start.1
  807.9 22.5 %collective-permute-start.2 = (bf16[1,256,1024]{1,2,0:T(8,128)(2,1)}, bf16[1,256,1024]{1,2,0:T(8,128)(2,1)}, u32[]{:S(2)}, u32[]{:S(2)}) collective-permute-start(bf16[1,256,1024]{1,2,0:T(8,128)(2,1)} %fusion.237), channel_id=1, source_target_pairs={{28,0},{0,4},{4,8},{8,12},{12,16},{16,20},{20,24},{24,28},{29,1},{... | collective-permute-start | bytes 1572872 | tf_op jit(solution)/shard_map/while/body/eval_jaxpr/ppermute | solution.py:32
  812.8 19.7 %collective-permute-start.3 = (bf16[1,256,1024]{1,2,0:T(8,128)(2,1)}, bf16[1,256,1024]{1,2,0:T(8,128)(2,1)}, u32[]{:S(2)}, u32[]{:S(2)}) collective-permute-start(bf16[1,256,1024]{1,2,0:T(8,128)(2,1)} %fusion.239), channel_id=1, source_target_pairs={{28,0},{0,4},{4,8},{8,12},{12,16},{16,20},{20,24},{24,28},{29,1},{... | collective-permute-start | bytes 1572872 | tf_op jit(solution)/shard_map/while/body/eval_jaxpr/ppermute | solution.py:32
  815.3 19.3 collective-permute-start
  822.4 12.2 collective-permute-start.1
  860.2 251.3 %all-reduce.6.cloned.1.call-start = ((), (), s32[]{:S(2)}) async-start(), calls=%async_computation.3 | async-start | bytes 196608 | tf_op jit(solution)/shard_map/psum | solution.py:442
  863.5 73.8 %copy-start.71 = (f32[1024]{0:T(1024)S(1)}, f32[1024]{0:T(1024)}, u32[]{:S(2)}) copy-start(f32[1024]{0:T(1024)} %convert_reduce_fusion.2) | copy-start | bytes 12292
  863.5 73.8 %copy-start.72 = (f32[1024]{0:T(1024)S(1)}, f32[1024]{0:T(1024)}, u32[]{:S(2)}) copy-start(f32[1024]{0:T(1024)} %get-tuple-element.678) | copy-start | bytes 12292
  863.5 73.8 %copy-start.82 = (f32[1024]{0:T(1024)S(1)}, f32[1024]{0:T(1024)}, u32[]{:S(2)}) copy-start(f32[1024]{0:T(1024)} %get-tuple-element.608) | copy-start | bytes 12292
  863.5 73.8 %copy-start.83 = (f32[1024]{0:T(1024)S(1)}, f32[1024]{0:T(1024)}, u32[]{:S(2)}) copy-start(f32[1024]{0:T(1024)} %get-tuple-element.617) | copy-start | bytes 12292
  863.5 75.8 %copy-start.53 = (bf16[1,40,1024]{2,1,0:T(8,128)(2,1)S(1)}, bf16[1,40,1024]{2,1,0:T(8,128)(2,1)}, u32[]{:S(2)}) copy-start(bf16[1,40,1024]{2,1,0:T(8,128)(2,1)} %param.17) | copy-start | bytes 245764
  939.3 983.5 %reduce-scatter.2.cloned.1.call-start = ((), (), s32[]{:S(2)}) async-start(), calls=%async_computation.2 | async-start | bytes 103809024 | tf_op jit(solution)/shard_map/reduce_scatter | solution.py:417
  964.0 65.6 %copy-start.89 = (pred[96]{0:T(512)(128)(4,1)S(1)}, pred[96]{0:T(512)(128)(4,1)}, u32[]{:S(2)}) copy-start(pred[96]{0:T(512)(128)(4,1)} %get-tuple-element.749) | copy-start | bytes 292
  (123 other events, 775.0 us)
Sparse Core Ops, SparseCore 0:
  11.5 278.2 all-gather.5
  350.0 37.5 all-gather.9
  390.1 36.7 all-gather.7
  860.3 74.5 all-reduce.7
  940.9 120.1 all-reduce.5
  1096.2 826.4 reduce-scatter.1
where the time goes:
time: 1950 us; the launch traced here: 1940 us
  waiting for transfers between devices  1190 us (61%)
  matrix products  200 us (10%)
  local copies, waits for them, and re-layouts  194 us (10%)
  other arithmetic  187 us (10%)
  starting transfers between devices  131 us (7%)
    reduce_scatter x1, waiting for transfers between devices, local(): lax.psum_scatter(jnp.where(occupied[:, None, None], jnp.take(grad_units,...  808 us
    all_gather x1, waiting for transfers between devices, local(): lax.all_gather(master.astype(jnp.bfloat16), ('seq', 'grp'), axis=0, tiled...  278 us
    ppermute x16, starting transfers between devices, passed_along(): return lax.ppermute(block, axis, route)  74 us
    unnamed x7, waiting for transfers between devices  68.9 us
    select_n x1, other arithmetic, local(): jnp.where(occupied[:, None, None], jnp.take(grad_units, unit_at, axis=0),...  66.4 us
    gather x1, local copies, waits for them, and re-layouts, local(): jnp.take(grad_units, unit_at, axis=0)  65.6 us
    ppermute x16, starting transfers between devices, shifted(): return lax.ppermute(block, axis, route)  56.3 us
  transfers between devices with their start and end apart: 38, of which 5 were waited for; matrix products, arithmetic and copies ran while one was open for 14% of the time, Pallas kernels for 0%

commit v1 on v0

v1 whole, which is shorter than its diff:
```python
import functools

import jax
import jax.numpy as jnp
from jax import lax
from jax.experimental import pallas as pl
from jax.experimental.pallas import tpu as pltpu
from jax.sharding import PartitionSpec as P

D = 1024
FF = 4096
HEADS = 16
HDIM = 64
STEP = 10


NEG_FILL = -1e30
NORM_EPS = 1e-05
BETA_ONE = 0.5
BETA_TWO = 0.75
RATE_MATRIX = 0.03
RATE_VECTOR = 0.4
WEIGHT_DECAY = 0.01
ADAM_EPS = 1e-08

BF16 = jnp.bfloat16
F32 = jnp.float32
LANES = 128
GROUP_UNITS = 4
GATHER_LIGHT = 4
REDUCE_LIGHT = 4
MIB = 1 << 20


def product(left, right):
    return jnp.dot(left, right, preferred_element_type=F32)


def product_tn(left, right):
    return jnp.einsum("rd,re->de", left, right, preferred_element_type=F32)


def product_nt(left, right):
    return jnp.einsum("rd,ed->re", left, right, preferred_element_type=F32)


def slot_tables(owners, slot_count, holders):
    unit_count = owners.shape[0]
    positions = lax.iota(jnp.int32, unit_count)
    same_owner = owners[None, :] == owners[:, None]
    slot_rank = jnp.sum(
        (same_owner & (positions[None, :] < positions[:, None])).astype(jnp.int32), axis=1
    )
    placed = owners * slot_count + slot_rank
    slot_ids = lax.iota(jnp.int32, holders * slot_count)
    matches = slot_ids[:, None] == placed[None, :]
    occupied = jnp.sum(matches.astype(jnp.int32), axis=1) > 0
    unit_at = jnp.sum(jnp.where(matches, positions[None, :], 0), axis=1)
    return (placed, unit_at, occupied)


def norm_forward(stream, gain_row, shift_row):
    row_mean = jnp.mean(stream, axis=-1, keepdims=True)
    centered = stream - row_mean
    inverse = lax.rsqrt(jnp.mean(centered * centered, axis=-1, keepdims=True) + NORM_EPS)
    normal_form = centered * inverse
    return (normal_form * gain_row + shift_row, normal_form, inverse)


def norm_backward(upstream, normal_form, inverse, gain_row):
    scaled = upstream * gain_row
    first_term = jnp.mean(scaled, axis=-1, keepdims=True)
    second_term = jnp.mean(scaled * normal_form, axis=-1, keepdims=True)
    grad_in = inverse * (scaled - first_term - normal_form * second_term)
    return (grad_in, jnp.sum(upstream * normal_form, axis=0), jnp.sum(upstream, axis=0))


def gelu_exact(values):
    return jax.nn.gelu(values, approximate=False)


def adam_step(weight, first, second_in, upstream, rate, decay):
    first_new = BETA_ONE * first + (1.0 - BETA_ONE) * upstream
    second_new = BETA_TWO * second_in + (1.0 - BETA_TWO) * upstream * upstream
    first_hat = first_new / (1.0 - BETA_ONE**STEP)
    second_hat = second_new / (1.0 - BETA_TWO**STEP)
    weight_new = weight - rate * (first_hat / (jnp.sqrt(second_hat) + ADAM_EPS) + decay * weight)
    return (first_new, second_new, weight_new)


def remote(src, dst, send_sem, recv_sem, target):
    return pltpu.make_async_remote_copy(
        src_ref=src,
        dst_ref=dst,
        send_sem=send_sem,
        recv_sem=recv_sem,
        device_id=target,
        device_id_type=pl.DeviceIdType.MESH,
    )


def greet_all(me, total, target_of):
    barrier = pltpu.get_barrier_semaphore()

    def signal(step, carry):
        pl.semaphore_signal(
            barrier,
            inc=1,
            device_id=target_of(lax.rem(me + step, total)),
            device_id_type=pl.DeviceIdType.MESH,
        )
        return carry

    lax.fori_loop(1, total, signal, 0)
    pl.semaphore_wait(barrier, total - 1)


class Place:
    def __init__(self, planes):
        self.seq = lax.axis_index("seq")
        self.z = lax.axis_index("grp")
        self.planes = planes
        self.core = lax.rem(self.seq, 2)
        self.x = lax.rem(lax.div(self.seq, 2), 2)
        self.y = lax.div(self.seq, 4)

    def at(self, core, x, y, z):
        return (y * 4 + x * 2 + core, z)

    def sibling(self):
        return self.at(1 - self.core, self.x, self.y, self.z)

    def x_peer(self):
        return self.at(self.core, 1 - self.x, self.y, self.z)

    def y_peer(self):
        return self.at(self.core, self.x, 1 - self.y, self.z)

    def above(self):
        return (self.seq, self.z + 1)

    def below(self):
        return (self.seq, self.z - 1)

    def peers(self, half):
        return (self.x_peer(), self.y_peer()) if half == 0 else (self.y_peer(), self.x_peer())

    def bits(self, half):
        return (self.y, self.x) if half == 0 else (self.x, self.y)


def tile_of(device, planes, half, unit_rows):
    seq, z = lax.div(device, planes), lax.rem(device, planes)
    core, x, y = lax.rem(seq, 2), lax.rem(lax.div(seq, 2), 2), lax.div(seq, 4)
    wide, narrow = jnp.where(half == 0, y, x), jnp.where(half == 0, x, y)
    half_rows = unit_rows // 2
    block = half_rows // planes
    first_row = pl.multiple_of(half * half_rows + z * block, block)
    first_column = pl.multiple_of((core * 4 + wide * 2 + narrow) * LANES, LANES)
    return (pl.ds(first_row, block), pl.ds(first_column, LANES))


def loop(first, last, work):
    def one(index, carry):
        work(index)
        return carry

    lax.fori_loop(first, last, one, 0)


class Gather:
    def __init__(self, planes, own_ref, whole_ref, own_sem, z_send, z_recv, p_send, p_recv):
        self.place = Place(planes)
        self.planes = planes
        self.z = self.place.z
        self.own_ref, self.whole_ref = own_ref, whole_ref
        self.own_sem = own_sem
        self.z_send, self.z_recv = z_send, z_recv
        self.p_send, self.p_recv = p_send, p_recv
        self.groups = whole_ref.shape[0]
        self.split = GATHER_LIGHT
        self.leave = 1 + 2 * (planes - 1)
        self.arrived = self.leave + 3

    def block(self, g, half, plane):
        wide, narrow = self.place.bits(half)
        first = self.place.core * 4 + wide * 2 + narrow
        return self.whole_ref.at[g, half, first, plane]

    def pair(self, g, half, plane):
        wide, narrow = self.place.bits(half)
        return self.whole_ref.at[g, half, pl.ds(self.place.core * 4 + wide * 2, 2), plane]

    def line(self, g, half, way, hop, plane, light):
        ref = self.block(g, half, plane) if light else self.pair(g, half, plane)
        return remote(
            self.own_ref.at[g, half] if light and hop == 0 else ref,
            ref,
            self.z_send.at[g, half, way, hop],
            self.z_recv.at[g, half, way, hop],
            self.place.above() if way == 0 else self.place.below(),
        )

    def planar(self, g, half, order, light, arriving=False):
        wide, narrow = self.place.bits(half)
        core = self.place.core
        if order == 0:
            first = core * 4 + wide * 2 + (1 - narrow if arriving else narrow)
            if light:
                ref = src = self.whole_ref.at[g, half, first]
            else:
                ref = self.whole_ref.at[g, half, first, self.z]
                src = self.own_ref.at[g, half]
        else:
            if order == 1:
                first, columns = core * 4 + (1 - wide if arriving else wide) * 2, 2
            else:
                first, columns = (1 - core if arriving else core) * 4, 4
            ref = src = self.whole_ref.at[g, half, pl.ds(first, columns)]
        target = self.place.peers(half)[order] if order < 2 else self.place.sibling()
        return remote(
            src, ref, self.p_send.at[g, half, order], self.p_recv.at[g, half, order], target
        )

    def own_copy(self, g, half):
        return pltpu.make_async_copy(
            self.own_ref.at[g, half],
            self.block(g, half, self.z),
            self.own_sem.at[g, half],
        )

    def enter_line(self, g, half, light):
        z = self.z

        @pl.when(z < self.planes - 1)
        def _():
            self.line(g, half, 0, 0, z, light).start()

        @pl.when(z > 0)
        def _():
            self.line(g, half, 1, 0, z, light).start()

    def hop(self, g, half, k, light):
        z, planes = self.z, self.planes

        @pl.when(z >= k)
        def _():
            self.line(g, half, 0, k - 1, z - k, light).wait_recv()

        if k < planes - 1:

            @pl.when((z >= k) & (z < planes - 1))
            def _():
                self.line(g, half, 0, k, z - k, light).start()

        @pl.when(z + k < planes)
        def _():
            self.line(g, half, 1, k - 1, z + k, light).wait_recv()

        if k < planes - 1:

            @pl.when((z + k < planes) & (z > 0))
            def _():
                self.line(g, half, 1, k, z + k, light).start()

    def exchange(self, g, half, order, light):
        self.planar(g, half, order, light, arriving=True).wait_recv()
        if order < 2:
            self.planar(g, half, order + 1, light).start()

    def heavy_start(self, g, half):
        self.own_copy(g, half).start()
        self.planar(g, half, 0, False).start()

    def heavy_enter(self, g, half):
        self.own_copy(g, half).wait()
        self.planar(g, half, 0, False, arriving=True).wait_recv()
        self.enter_line(g, half, False)

    def heavy_leave(self, g, half):
        self.hop(g, half, self.planes - 1, False)
        self.planar(g, half, 1, False).start()

    def light_start(self, g, half):
        self.own_copy(g, half).start()
        self.enter_line(g, half, True)

    def light_leave(self, g, half):
        self.hop(g, half, self.planes - 1, True)
        self.own_copy(g, half).wait()
        self.planar(g, half, 0, True).start()

    def tick(self, t):
        planes, leave = self.planes, self.leave

        def during(lag, action, first, last):
            g = t - lag

            @pl.when((g >= first) & (g < last))
            def _():
                for half in range(2):
                    action(g, half)

        def heavy(lag, action):
            during(lag, action, self.split, self.groups)

        def light(lag, action):
            during(lag, action, 0, self.split)

        during(leave + 3, lambda g, half: self.exchange(g, half, 2, False), 0, self.groups)
        during(leave + 2, lambda g, half: self.exchange(g, half, 1, False), 0, self.groups)
        heavy(leave, self.heavy_leave)
        light(leave, lambda g, half: self.exchange(g, half, 0, True))
        for k in reversed(range(1, planes - 1)):
            heavy(1 + 2 * k, lambda g, half, k=k: self.hop(g, half, k, False))
        light(leave - 2, self.light_leave)
        for k in reversed(range(1, planes - 1)):
            light(1 + k, lambda g, half, k=k: self.hop(g, half, k, True))
        heavy(1, self.heavy_enter)
        heavy(0, self.heavy_start)
        light(0, self.light_start)

    def drain(self):
        z, planes = self.z, self.planes

        def one(g, light):
            for half in range(2):
                for k in range(planes - 1):

                    @pl.when((z >= k) & (z < planes - 1))
                    def _(half=half, k=k):
                        self.line(g, half, 0, k, z - k, light).wait_send()

                    @pl.when((z + k < planes) & (z > 0))
                    def _(half=half, k=k):
                        self.line(g, half, 1, k, z + k, light).wait_send()

                for order in range(3):
                    self.planar(g, half, order, light).wait_send()

        loop(0, self.split, lambda g: one(g, True))
        loop(self.split, self.groups, lambda g: one(g, False))


def gather_scratch(planes, groups):
    dma = pltpu.SemaphoreType.DMA
    return [
        dma((groups, 2)),
        dma((groups, 2, 2, planes - 1)),
        dma((groups, 2, 2, planes - 1)),
        dma((groups, 2, 3)),
        dma((groups, 2, 3)),
    ]


NORM_ROWS = 32


def norm_into(stream_ref, gain_row, shift_row, out_ref):
    def one(block):
        span = pl.ds(pl.multiple_of(block * NORM_ROWS, NORM_ROWS), NORM_ROWS)
        normed = norm_forward(stream_ref[span].astype(F32), gain_row, shift_row)[0]
        out_ref[span] = normed.astype(BF16)

    loop(0, out_ref.shape[0] // NORM_ROWS, one)


def weight_block(weight_ref, slot, block, unit):
    halves, planes = weight_ref.shape[1], weight_ref.shape[3]
    return [weight_ref[slot, h, block, p, unit] for h in range(halves) for p in range(planes)]


def dot_tiles(left, weight_ref, slot, emit, turned=False, unrolled=False):
    blocks, units = weight_ref.shape[2], weight_ref.shape[4]

    def one(j, carry):
        if turned:
            weight = jnp.concatenate(
                [jnp.concatenate(weight_block(weight_ref, slot, b, j), 0) for b in range(blocks)], 1
            )
            emit(j, dot_nt(left, weight))
        else:
            weight = jnp.concatenate(
                [
                    jnp.concatenate(
                        sum(
                            (weight_block(weight_ref, slot, 2 * j + b, u) for u in range(units)),
                            [],
                        ),
                        0,
                    )
                    for b in range(2)
                ],
                1,
            )
            emit(j, dot_nn(left, weight))
        return carry

    if unrolled:
        for j in range(4):
            one(j, 0)
    else:
        lax.fori_loop(0, 4, one, 0)


TRAVEL = (0, 1, 2, 3, 5, 6, 4, 7, 8, 9, 10, 11, 12, 13, 14, 15)
REDUCE = (12, 13, 14, 15, 8, 9, 10, 11, 7, 4, 3, 5, 6, 0, 1, 2)


def tables_kernel(slots, owners_ref, holder_ref, slot_ref, group_ref, unit_ref, count):
    holders = count.shape[0]

    def clear(n, carry):
        count[n] = 0
        for s in range(slots):
            group_ref[n * slots + s] = -1
            unit_ref[n * slots + s] = 0
        return carry

    lax.fori_loop(0, holders, clear, 0)
    for unit in range(owners_ref.shape[0]):
        matrix, part = divmod(unit, GROUP_UNITS)
        owner = owners_ref[unit]
        slot = count[owner]
        count[owner] = slot + 1
        travel = TRAVEL.index(matrix) * GROUP_UNITS + part
        holder_ref[travel] = owner
        slot_ref[travel] = slot
        group_ref[owner * slots + slot] = REDUCE.index(matrix)
        unit_ref[owner * slots + slot] = part


def owner_tables(owners, slots, holders):
    units = owners.shape[0]
    smem = pl.BlockSpec(memory_space=pltpu.SMEM)
    return pl.pallas_call(
        functools.partial(tables_kernel, slots),
        out_shape=(jax.ShapeDtypeStruct((units,), jnp.int32),) * 2
        + (jax.ShapeDtypeStruct((holders * slots,), jnp.int32),) * 2,
        in_specs=[smem],
        out_specs=(smem,) * 4,
        scratch_shapes=[pltpu.SMEM((holders,), jnp.int32)],
        name="owner_tables",
    )(owners)


def forward_kernel(
    seqs,
    planes,
    window_ref,
    length_ref,
    holder_ref,
    slot_ref,
    master_ref,
    tokens_ref,
    memory_ref,
    vectors_ref,
    whole_ref,
    h1_ref,
    joined_ref,
    qkv_all,
    rounded,
    log_ref,
    x2_ref,
    h2_ref,
    cq_ref,
    mem_ref,
    crossed_low_ref,
    cross_log_ref,
    x3_ref,
    h3_ref,
    act_ref,
    slope_ref,
    mixed_ref,
    master_wide,
    master_low,
    tiles,
    own,
    memory_came,
    memory_wide,
    memory_all,
    weights,
    qkv_out,
    down,
    own_sem,
    z_send,
    z_recv,
    p_send,
    p_recv,
    load_sem,
    master_sem,
    tile_send,
    tile_recv,
    memory_send,
    memory_recv,
    send_sem,
    recv_sem,
    back_send,
    back_recv,
):
    fetch = pltpu.make_async_copy(master_ref, master_wide, master_sem)
    fetch.start()
    gather = Gather(planes, own, whole_ref, own_sem, z_send, z_recv, p_send, p_recv)
    place = gather.place
    me, z = place.seq, place.z
    rows = tokens_ref.shape[0]
    width = D // seqs
    tile = 2 * LANES
    total = seqs * planes
    here = me * planes + z
    mem_rows = memory_all.shape[0] // seqs
    greet_all(here, total, lambda j: (lax.div(j, planes), lax.rem(j, planes)))

    def vector(index):
        return vectors_ref[index : index + 1]

    def columns_of(j):
        return pl.ds(pl.multiple_of(j * tile, tile), tile)

    def tile_copy(peer, slot, half):
        tile_rows, tile_columns = tile_of(peer, planes, half, master_low.shape[1])
        return remote(
            master_low.at[:, tile_rows, tile_columns],
            tiles.at[slot, half],
            tile_send.at[peer, half],
            tile_recv.at[slot, half],
            (lax.div(peer, planes), lax.rem(peer, planes)),
        )

    def memory_copy(peer, slot):
        return remote(
            memory_ref, memory_came.at[slot], memory_send.at[peer], memory_recv.at[slot], (peer, z)
        )

    def spread():
        fetch.wait()
        part = 64

        def lower(index):
            slot, block = lax.div(index, master_low.shape[1] // part), lax.rem(
                index, master_low.shape[1] // part
            )
            span = pl.ds(pl.multiple_of(block * part, part), part)
            master_low[slot, span] = master_wide[slot, span].astype(BF16)

        loop(0, master_low.shape[0] * master_low.shape[1] // part, lower)

        def start(step):
            peer = lax.rem(here + step, total)
            loop(0, 2, lambda half: tile_copy(peer, here, half).start())

        loop(1, total, start)
        loop(1, seqs, lambda step: memory_copy(lax.rem(me + step, seqs), me).start())

        def keep_own(half):
            tile_rows, tile_columns = tile_of(here, planes, half, master_low.shape[1])
            tiles[here, half] = master_low[:, tile_rows, tile_columns]

        loop(0, 2, keep_own)
        memory_came[me] = memory_ref[...]
        norm_into(tokens_ref, vector(0), vector(1), h1_ref)

        def finish_memory(step):
            peer = lax.rem(me + step, seqs)
            memory_copy(peer, peer).wait()

        loop(1, seqs, finish_memory)

        def widen(j):
            span = pl.ds(pl.multiple_of(j * mem_rows, 8), mem_rows)
            memory_wide[span] = memory_came[j].astype(F32)[:mem_rows]

        loop(0, seqs, widen)

        def narrow(block):
            span = pl.ds(pl.multiple_of(block * part, part), part)
            memory_all[span] = memory_wide[span].astype(BF16)

        loop(0, memory_all.shape[0] // part, narrow)

        def finish(step):
            peer = lax.rem(here + total - step, total)
            loop(0, 2, lambda half: tile_copy(peer, peer, half).wait())

        loop(1, total, finish)

        def keep(unit):
            g, u = lax.div(unit, GROUP_UNITS), lax.rem(unit, GROUP_UNITS)
            for half in range(2):
                own[g, half, u] = tiles[holder_ref[unit], half, slot_ref[unit]]

        loop(0, holder_ref.shape[0], keep)

    def load(position, slot):
        return pltpu.make_async_copy(whole_ref.at[position], weights.at[slot], load_sem.at[slot])

    def outward(part, peer, slot):
        return remote(
            qkv_out.at[part, peer],
            qkv_all.at[part, slot],
            send_sem.at[part, peer],
            recv_sem.at[part, slot],
            (peer, z),
        )

    def backward_copy(peer, slot):
        return remote(
            rounded.at[peer],
            joined_ref.at[:, pl.ds(pl.multiple_of(slot * width, width), width)],
            back_send.at[peer],
            back_recv.at[slot],
            (peer, z),
        )

    def project(part):
        load(part, part).start()
        load(part, part).wait()
        bias_row = 6 + lax.div(part, 2)

        def emit(j, result):
            bias = vectors_ref[pl.ds(bias_row, 1), columns_of(j)]
            result = (result + jnp.where(part == 1, 0.0, bias)).astype(BF16)
            for piece in range(tile // width):
                qkv_out[part, j * (tile // width) + piece] = result[
                    :, piece * width : (piece + 1) * width
                ]

        dot_tiles(h1_ref[...], weights, part, emit, unrolled=True)
        loop(1, seqs, lambda step: outward(part, lax.rem(me + step, seqs), me).start())
        qkv_all[part, me] = qkv_out[part, me]

    head_count = width // HDIM

    def query_block(i):
        def arrive(ahead):
            @pl.when((lax.rem(i, 2) == 0) & (i + ahead != me))
            def _():
                loop(0, 3, lambda part: outward(part, i + ahead, i + ahead).wait_recv())

        loop(0, 2, arrive)
        rounded[i] = attend_pairs(i, rows, head_count, window_ref[0], qkv_all, log_ref).astype(BF16)

        @pl.when(i != me)
        def _():
            backward_copy(i, me).start()

        @pl.when(i == me)
        def _():
            joined_ref[:, pl.ds(pl.multiple_of(i * width, width), width)] = rounded[i]

    def after_self():
        def arrive(step):
            peer = lax.rem(me + step, seqs)
            backward_copy(peer, peer).wait_recv()

        loop(1, seqs, arrive)
        load(3, 0).wait()

        def emit(j, result):
            columns = columns_of(j)
            x2_ref[:, columns] = (
                tokens_ref[:, columns].astype(F32) + result + vectors_ref[8:9, columns]
            )

        dot_tiles(joined_ref[...], weights, 0, emit, unrolled=True)
        norm_into(x2_ref, vector(2), vector(3), h2_ref)
        load(6, 1).wait()

        def emit_query(j, result):
            columns = columns_of(j)
            cq_ref[:, columns] = (result + vectors_ref[9:10, columns]).astype(BF16)

        dot_tiles(h2_ref[...], weights, 1, emit_query, unrolled=True)

    def memory_rows(part):
        load(4 + part, part).start()
        load(4 + part, part).wait()

        def emit(j, result):
            columns = columns_of(j)
            bias = jnp.where(part == 1, vectors_ref[10:11, columns], 0.0)
            mem_ref[part, :, columns] = (result + bias).astype(BF16)

        dot_tiles(memory_all[...], weights, part, emit, unrolled=True)

    def cross_blocks(first, last):
        def one(j):
            columns = pl.ds(pl.multiple_of(j * LANES, LANES), LANES)
            crossed, logs = cross_attend(
                length_ref[0], cq_ref[:, columns], mem_ref[0, :, columns], mem_ref[1, :, columns]
            )
            for head in range(len(logs)):
                cross_log_ref[j, head : head + 1] = logs[head]
            crossed_low_ref[:, columns] = crossed.astype(BF16)

        loop(first, last, one)

    def after_cross():
        load(7, 2).wait()

        def emit(j, result):
            columns = columns_of(j)
            total = x2_ref[:, columns] + result + vectors_ref[11:12, columns]
            x3_ref[:, columns] = total
            down[:, columns] = total + vectors_ref[12 + FF // D : 13 + FF // D, columns]

        dot_tiles(crossed_low_ref[...], weights, 2, emit, unrolled=True)
        norm_into(x3_ref, vector(4), vector(5), h3_ref)

    def hidden_up(j):
        slot = lax.rem(j + 3, 4)
        load(8 + j, slot).wait()

        def emit(r, result):
            columns = columns_of(r)
            spread = pl.ds(pl.multiple_of(j * D + r * tile, tile), tile)
            pre = result + vectors_ref[pl.ds(12 + j, 1), columns]
            cumulative = 0.5 * (1.0 + lax.erf(pre * 0.5**0.5))
            density = jnp.exp(-0.5 * pre * pre) * (2.0 * jnp.pi) ** -0.5
            act_ref[:, spread] = (pre * cumulative).astype(BF16)
            slope_ref[:, spread] = (cumulative + pre * density).astype(BF16)

        dot_tiles(h3_ref[...], weights, slot, emit, turned=True, unrolled=True)

        @pl.when(j < 3)
        def _():
            load(12 + j, slot).start()

    def hidden_down(j):
        slot = lax.rem(j + 3, 4)
        load(12 + j, slot).wait()
        left = act_ref[:, pl.ds(pl.multiple_of(j * D, D), D)]

        def emit(r, result):
            columns = columns_of(r)
            down[:, columns] = down[:, columns] + result

        dot_tiles(left, weights, slot, emit, unrolled=True)

    arrived = gather.arrived

    def tick(t):
        gather.tick(t)

        @pl.when((t >= arrived) & (t < arrived + 3))
        def _():
            project(t - arrived)

        first_block = arrived + 3

        @pl.when((t >= first_block) & (t < first_block + seqs))
        def _():
            query_block(t - first_block)

        @pl.when((t >= arrived + 4) & (t < arrived + 6))
        def _():
            memory_rows(t - arrived - 4)

        early = arrived + 6
        for step, (position, slot) in enumerate(((3, 0), (6, 1), (7, 2), (8, 3))):

            @pl.when(t == early + step)
            def _(position=position, slot=slot):
                load(position, slot).start()

        late = first_block + seqs

        @pl.when(t == late)
        def _():
            after_self()
            load(9, 0).start()
            load(10, 1).start()

        @pl.when((t >= late) & (t < late + 2))
        def _():
            cross_blocks(4 * (t - late), 4 * (t - late) + 4)

        @pl.when(t == late + 1)
        def _():
            after_cross()
            load(11, 2).start()

        hidden = late + 2

        @pl.when((t >= hidden) & (t < hidden + 2))
        def _():
            loop(2 * (t - hidden), 2 * (t - hidden) + 2, hidden_up)

        @pl.when(t == hidden + 2)
        def _():
            load(15, 2).start()

        @pl.when(t > hidden)
        def _():
            loop(jnp.where(t == hidden + 1, 0, 1), jnp.where(t == hidden + 1, 1, 4), hidden_down)

    spread()
    loop(0, gather.groups + arrived, tick)

    def close(block):
        span = pl.ds(pl.multiple_of(block * NORM_ROWS, NORM_ROWS), NORM_ROWS)
        mixed_ref[span] = down[span].astype(BF16)

    loop(0, rows // NORM_ROWS, close)

    def finish(step):
        peer = lax.rem(me + step, seqs)
        loop(0, 3, lambda part: outward(part, peer, me).wait_send())
        backward_copy(peer, me).wait_send()

    loop(1, seqs, finish)
    gather.drain()


def forward_pass(
    seqs, planes, windows, lengths, holder, slot, master, tokens, memory, mem, vectors
):
    groups = holder.shape[0] // GROUP_UNITS
    slots, unit_rows = master.shape[:2]
    block = (unit_rows // 2 // planes, LANES)
    matrix = (2, D // LANES, planes, GROUP_UNITS) + block
    rows = tokens.shape[0]
    width = D // seqs
    dma = pltpu.SemaphoreType.DMA
    vmem = pl.BlockSpec(memory_space=pltpu.VMEM)
    smem = pl.BlockSpec(memory_space=pltpu.SMEM)
    anywhere = pl.BlockSpec(memory_space=pl.ANY)
    shape = jax.ShapeDtypeStruct
    by_head = (seqs, rows, width)
    outs = (
        shape((groups,) + matrix, BF16),
        shape((rows, D), BF16),
        shape((rows, D), BF16),
        shape((3,) + by_head, BF16),
        shape(by_head, BF16),
        shape((seqs, 8, rows), F32),
        shape((rows, D), F32),
        shape((rows, D), BF16),
        shape((rows, D), BF16),
        shape((2, mem, D), BF16),
        shape((rows, D), BF16),
        shape((D // LANES, 8, rows), F32),
        shape((rows, D), F32),
        shape((rows, D), BF16),
        shape((rows, FF), BF16),
        shape((rows, FF), BF16),
        shape((rows, D), BF16),
    )
    return pl.pallas_call(
        functools.partial(forward_kernel, seqs, planes),
        out_shape=outs,
        in_specs=[smem] * 4 + [anywhere, vmem, vmem, vmem],
        out_specs=(anywhere,) + (vmem,) * (len(outs) - 1),
        scratch_shapes=[
            pltpu.VMEM(master.shape, F32),
            pltpu.VMEM(master.shape, BF16),
            pltpu.VMEM((seqs * planes, 2, slots) + block, BF16),
            pltpu.VMEM((groups, 2, GROUP_UNITS) + block, BF16),
            pltpu.VMEM((seqs,) + memory.shape, BF16),
            pltpu.VMEM((mem, D), F32),
            pltpu.VMEM((mem, D), BF16),
            pltpu.VMEM((4,) + matrix, BF16),
            pltpu.VMEM((3,) + by_head, BF16),
            pltpu.VMEM((rows, D), F32),
        ]
        + gather_scratch(planes, groups)
        + [
            dma((4,)),
            dma(()),
            dma((seqs * planes, 2)),
            dma((seqs * planes, 2)),
            dma((seqs,)),
            dma((seqs,)),
        ]
        + [dma((3, seqs)), dma((3, seqs)), dma((seqs,)), dma((seqs,))],
        compiler_params=pltpu.CompilerParams(
            collective_id=2, has_side_effects=True, vmem_limit_bytes=56 * MIB
        ),
        name="forward_pass",
    )(windows, lengths, holder, slot, master, tokens, memory, vectors)


GRAD_SLOTS = 4
COLUMN_SLOTS = 8


class Reduce:
    def __init__(
        self,
        planes,
        made,
        theirs_far,
        wide_far,
        chain_far,
        sums_ref,
        theirs,
        wide_in,
        narrow_in,
        narrow_all,
        column,
        chain_in,
        light_in,
        load_sem,
        chain_sem,
        c_send,
        c_recv,
        p_send,
        p_recv,
        z_send,
        z_recv,
    ):
        self.place = Place(planes)
        self.planes = planes
        self.z = self.place.z
        self.made = made
        self.theirs_far, self.wide_far, self.chain_far = theirs_far, wide_far, chain_far
        self.sums_ref = sums_ref
        self.theirs, self.wide_in = theirs, wide_in
        self.narrow_in, self.column, self.chain_in = narrow_in, column, chain_in
        self.narrow_all, self.light_in = narrow_all, light_in
        self.load_sem, self.chain_sem = load_sem, chain_sem
        self.c_send, self.c_recv = c_send, c_recv
        self.p_send, self.p_recv = p_send, p_recv
        self.z_send, self.z_recv = z_send, z_recv
        self.groups = theirs_far.shape[0]
        self.enter = 3
        self.leave = self.enter + 2 * (planes - 1)
        self.last = self.leave + 1
        self.split = self.groups - REDUCE_LIGHT
        self.light_enter = self.enter + 2

    def to_sibling(self, g):
        src = self.made.at[lax.rem(g, GRAD_SLOTS), :, pl.ds((1 - self.place.core) * 4, 4)]
        return remote(
            src, self.theirs_far.at[g], self.c_send.at[g], self.c_recv.at[g], self.place.sibling()
        )

    def planar(self, g, half, order, light=False):
        place = self.place
        wide, narrow = place.bits(half)
        narrow_peer, wide_peer = place.peers(half)
        if order == 0:
            slot = lax.rem(g, GRAD_SLOTS)
            src = self.made.at[slot, half, pl.ds(place.core * 4 + (1 - wide) * 2, 2)]
            dst, target = self.wide_far.at[g, half], wide_peer
        elif light:
            src = self.column.at[lax.rem(g, COLUMN_SLOTS), :, half, 1 - narrow]
            dst, target = self.narrow_all.at[g - self.split, half], narrow_peer
        else:
            src = self.column.at[lax.rem(g, COLUMN_SLOTS), self.z, half, 1 - narrow]
            dst, target = self.narrow_in.at[g, half], narrow_peer
        return remote(
            src, dst, self.p_send.at[g, half, order], self.p_recv.at[g, half, order], target
        )

    def load(self, g, order):
        src, dst = ((self.theirs_far, self.theirs), (self.wide_far, self.wide_in))[order]
        return pltpu.make_async_copy(src.at[g], dst, self.load_sem.at[order])

    def plane_at(self, way, reach):
        return reach if way == 0 else self.planes - 1 - reach

    def chain(self, g, way, reach, light):
        src = self.column.at[lax.rem(g, COLUMN_SLOTS), self.plane_at(way, reach)]
        dst = self.chain_far.at[g, way, reach - 1]
        return remote(
            src.at[:, 0] if light else src,
            dst.at[:, 0] if light else dst,
            self.z_send.at[g, way, reach - 1],
            self.z_recv.at[g, way, reach - 1],
            self.place.above() if way == 0 else self.place.below(),
        )

    def chain_load(self, g, way, reach, light):
        src = self.chain_far.at[g, way, reach - 1]
        dst = self.light_in if light else self.chain_in
        return pltpu.make_async_copy(
            src.at[:, 0] if light else src,
            dst.at[way, reach - 1],
            self.chain_sem.at[1 if light else 0, way, reach - 1],
        )

    def chain_of(self, t, way, action):
        here = self.z if way == 0 else self.planes - 1 - self.z
        for light in (False, True):
            lag = self.light_enter + here if light else self.enter + 2 * here
            g = t - lag
            first, last = (self.split, self.groups) if light else (0, self.split)

            @pl.when((here > 0) & (g >= first) & (g < last))
            def _(light=light, g=g):
                loop(here, self.planes, lambda reach: action(g, way, reach, light))

    def chain_arrive(self, g, way, reach, light):
        self.chain(g, way, reach, light).wait_recv()
        self.chain_load(g, way, reach, light).start()

    def chain_pass(self, g, way, reach, light):
        here = self.z if way == 0 else self.planes - 1 - self.z
        slot, plane = lax.rem(g, COLUMN_SLOTS), self.plane_at(way, reach)
        self.chain_load(g, way, reach, light).wait()
        if light:
            for half in range(2):
                self.column[slot, plane, half, 0] = (
                    self.column[slot, plane, half, 0] + self.light_in[way, reach - 1, half]
                )
        else:
            self.column[slot, plane] = self.column[slot, plane] + self.chain_in[way, reach - 1]

        @pl.when(reach > here)
        def _():
            self.chain(g, way, reach, light).start()

    def start_chains(self, g, light):
        for way in range(2):

            @pl.when(self.z == (0 if way == 0 else self.planes - 1))
            def _(way=way):
                loop(1, self.planes, lambda reach: self.chain(g, way, reach, light).start())

    def enter_line(self, g):
        slot, spot = lax.rem(g, GRAD_SLOTS), lax.rem(g, COLUMN_SLOTS)
        self.load(g, 1).wait()
        for half in range(2):
            wide, narrow = self.place.bits(half)
            first = self.place.core * 4 + wide * 2
            for b in range(2):
                total = self.made[slot, half, first + b] + self.wide_in[half, b]
                for plane in range(self.planes):
                    self.column[spot, plane, half, b] = total[plane]

        @pl.when(g < self.split)
        def _():
            self.start_chains(g, False)

        @pl.when(g >= self.split)
        def _():
            for half in range(2):
                self.planar(g, half, 1, True).start()

    def enter_light(self, g):
        slot = lax.rem(g, COLUMN_SLOTS)
        for half in range(2):
            wide, narrow = self.place.bits(half)
            self.planar(g, half, 1, True).wait()

            def one(plane, half=half, narrow=narrow):
                self.column[slot, plane, half, 0] = (
                    self.column[slot, plane, half, narrow]
                    + self.narrow_all[g - self.split, half, plane]
                )

            loop(0, self.planes, one)
        self.start_chains(g, True)

    def finish_light(self, g):
        slot = lax.rem(g, COLUMN_SLOTS)
        for half in range(2):
            self.sums_ref[g, half] = self.column[slot, self.z, half, 0]

    def finish(self, g):
        for half in range(2):
            wide, narrow = self.place.bits(half)
            self.planar(g, half, 1).wait_recv()
            own = self.column[lax.rem(g, COLUMN_SLOTS), self.z, half, narrow].astype(F32)
            self.sums_ref[g, half] = (own + self.narrow_in[g, half].astype(F32)).astype(BF16)

    def arrive(self, g, order):
        if order == 0:
            self.to_sibling(g).wait_recv()
        else:
            for half in range(2):
                self.planar(g, half, 0).wait_recv()
        self.load(g, order).start()

    def add(self, g):
        slot = lax.rem(g, GRAD_SLOTS)
        self.load(g, 0).wait()
        first = self.place.core * 4
        for half in range(2):
            for b in range(4):
                self.made[slot, half, first + b] = (
                    self.made[slot, half, first + b] + self.theirs[half, b]
                )
            self.planar(g, half, 0).start()

    def leave_line(self, g):
        for half in range(2):
            self.planar(g, half, 1).start()

    def wait_column_sends(self, g, light=False):
        if not light:
            for half in range(2):
                self.planar(g, half, 1).wait_send()
        for way in range(2):
            here = self.z if way == 0 else self.planes - 1 - self.z
            loop(here + 1, self.planes, lambda reach: self.chain(g, way, reach, light).wait_send())

    def wait_made_sends(self, g):
        self.to_sibling(g).wait_send()
        for half in range(2):
            self.planar(g, half, 0).wait_send()

    def during(self, t, lag, action, first=0, last=None):
        g = t - lag

        @pl.when((g >= first) & (g < (self.groups if last is None else last)))
        def _():
            action(g)

    def receive(self, t):
        self.during(t, 1, lambda g: self.arrive(g, 0))
        self.during(t, self.enter, lambda g: self.arrive(g, 1))
        for way in range(2):
            self.chain_of(t, way, self.chain_arrive)
        self.during(t, self.last, self.finish, 0, self.split)

        @pl.when((t >= GRAD_SLOTS) & (t < self.groups))
        def _():
            self.wait_made_sends(t - GRAD_SLOTS)

    def advance(self, t):
        self.during(t, 0, lambda g: self.to_sibling(g).start())
        for way in range(2):
            self.chain_of(t, way, self.chain_pass)
        self.during(t, self.leave, self.leave_line, 0, self.split)
        self.during(t, self.light_enter + self.planes, self.finish_light, self.split)
        self.during(t, self.light_enter, self.enter_light, self.split)

        @pl.when((t >= self.enter + COLUMN_SLOTS) & (t < self.enter + self.groups))
        def _():
            self.wait_column_sends(t - self.enter - COLUMN_SLOTS)

        self.during(t, self.enter, self.enter_line)
        self.during(t, 1, self.add)

    def drain(self):
        loop(self.groups - GRAD_SLOTS, self.groups, self.wait_made_sends)
        loop(self.groups - COLUMN_SLOTS, self.split, self.wait_column_sends)
        loop(self.split, self.groups, lambda g: self.wait_column_sends(g, True))


BACKWARD_READS = (12, 8, 13, 9, 14, 10, 15, 11, 7, 6, 3, 4, 5, 0, 1, 2)
READ_SLOTS = 3


def backward_kernel(
    seqs,
    planes,
    window_ref,
    length_ref,
    group_ref,
    unit_ref,
    whole_ref,
    slope_ref,
    cotangent_ref,
    tokens_ref,
    x2_ref,
    x3_ref,
    h1_ref,
    h2_ref,
    h3_ref,
    act_ref,
    crossed_ref,
    cq_ref,
    mem_ref,
    cross_log_ref,
    joined_ref,
    attended_ref,
    qkv_all,
    log_ref,
    memory_ref,
    vectors_ref,
    theirs_far,
    wide_far,
    chain_far,
    slots_ref,
    grad_tokens_ref,
    grad_memory_ref,
    vec_sum_ref,
    sums_ref,
    vec_ref,
    vec_part,
    vec_came,
    vec_planes,
    made,
    theirs,
    wide_in,
    narrow_in,
    narrow_all,
    column,
    chain_in,
    light_in,
    weights,
    dx,
    dh,
    du,
    dx3_low,
    dx2_low,
    dco,
    dcq,
    mem_parts,
    mem_theirs,
    mem_came,
    mem_low,
    do_all,
    delta,
    dq_total,
    dk_total,
    dv_total,
    dq_low,
    dk_low,
    dv_low,
    dq_back,
    dk_back,
    dv_back,
    load_sem,
    chain_sem,
    c_send,
    c_recv,
    p_send,
    p_recv,
    z_send,
    z_recv,
    read_sem,
    slope_sem,
    fold_send,
    fold_recv,
    mem_send,
    mem_recv,
    do_send,
    do_recv,
    back_send,
    back_recv,
    vec_send,
    vec_recv,
    across_send,
    across_recv,
    slot_send,
    slot_recv,
    own_sem,
):
    reduce = Reduce(
        planes,
        made,
        theirs_far,
        wide_far,
        chain_far,
        sums_ref,
        theirs,
        wide_in,
        narrow_in,
        narrow_all,
        column,
        chain_in,
        light_in,
        load_sem,
        chain_sem,
        c_send,
        c_recv,
        p_send,
        p_recv,
        z_send,
        z_recv,
    )
    place = reduce.place
    me, z = place.seq, place.z
    rows = tokens_ref.shape[0]
    width = D // seqs
    tile = 2 * LANES
    head_count = width // HDIM
    mem_rows = mem_ref.shape[1] // seqs
    padded = memory_ref.shape[0]
    ups = FF // D

    total = seqs * planes
    here = me * planes + z

    def read(k):
        slot = k % READ_SLOTS
        return pltpu.make_async_copy(
            whole_ref.at[BACKWARD_READS[k]], weights.at[slot], read_sem.at[slot]
        )

    def using(k, work):
        read(k).wait()
        work(k % READ_SLOTS)
        if k + READ_SLOTS < len(BACKWARD_READS):
            read(k + READ_SLOTS).start()

    greet_all(here, total, lambda j: (lax.div(j, planes), lax.rem(j, planes)))

    slope_copy = pltpu.make_async_copy(slope_ref, du, slope_sem)
    slope_copy.start()
    for k in range(READ_SLOTS):
        read(k).start()

    def columns_of(j, count=tile):
        return pl.ds(pl.multiple_of(j * count, count), count)

    def vector(index):
        return vectors_ref[index : index + 1]

    def row_sum(values):
        return jnp.sum(values.astype(F32), axis=0, keepdims=True)

    def norm_back(stream_ref, gain_row, base, out_ref, low_ref):
        gain = vector(gain_row)
        part = rows // 4

        def one(block, sums):
            span = pl.ds(pl.multiple_of(block * part, part), part)
            _, form, inverse = norm_forward(stream_ref[span].astype(F32), 1.0, 0.0)
            upstream = dh[span]
            scaled = upstream * gain
            first = jnp.mean(scaled, axis=-1, keepdims=True)
            second = jnp.mean(scaled * form, axis=-1, keepdims=True)
            total = base(span) + inverse * (scaled - first - form * second)
            out_ref[span] = total
            gains, shifts, lows = sums
            if low_ref is not None:
                low = total.astype(BF16)
                low_ref[span] = low
                lows = lows + row_sum(low)
            return (gains + row_sum(upstream * form), shifts + row_sum(upstream), lows)

        zero = jnp.zeros((1, D), F32)
        gains, shifts, lows = lax.fori_loop(0, 4, one, (zero, zero, zero))
        vec_ref[gain_row : gain_row + 1] = gains
        vec_ref[gain_row + 1 : gain_row + 2] = shifts
        return lows

    def grad_matrix(slot, left_ref, first_column, right_ref):
        def one(r):
            first = first_column + r * tile
            left = left_ref[:, pl.ds(pl.multiple_of(first, tile), tile)]
            block = made.shape[5]
            for c in range(2):
                columns = slice(c * (D // 2), (c + 1) * (D // 2))
                result = dot_tn(left, right_ref[:, columns]).astype(BF16)
                for part in range(tile // block):
                    for b in range(D // 2 // LANES):
                        made[slot, part // planes, c * 4 + b, part % planes, r] = result[
                            part * block : (part + 1) * block, b * LANES : (b + 1) * LANES
                        ]

        def two(pair):
            one(2 * pair)
            one(2 * pair + 1)

        loop(0, GROUP_UNITS // 2, two)

    def hidden_back(j):
        if j == 0:
            dh[...] = jnp.zeros_like(dh)
            slope_copy.wait()
            vec_ref[...] = jnp.zeros_like(vec_ref)

        def slopes(slot):
            def emit(r, result):
                spread = pl.ds(pl.multiple_of(j * D + r * tile, tile), tile)
                low = (result * du[:, spread].astype(F32)).astype(BF16)
                du[:, spread] = low
                vec_ref[12 + j : 13 + j, columns_of(r)] = row_sum(low)

            dot_tiles(cotangent_ref[...], weights, slot, emit, turned=True, unrolled=True)

        def inner(slot):
            def emit(r, result):
                dh[:, columns_of(r)] = dh[:, columns_of(r)] + result

            dot_tiles(du[:, j * D : (j + 1) * D], weights, slot, emit, unrolled=True)

        using(2 * j, slopes)
        using(2 * j + 1, inner)

    def mem_fold():
        return remote(
            mem_parts.at[1 - place.core],
            mem_theirs,
            fold_send,
            fold_recv,
            place.sibling(),
        )

    chip = lax.div(me, 2)
    chips = seqs // 2

    def mem_copy(peer, slot):
        return remote(
            mem_parts.at[place.core, peer],
            mem_came.at[slot],
            mem_send.at[peer],
            mem_recv.at[slot],
            (2 * peer + place.core, z),
        )

    def cross_branch():
        vec_ref[12 + ups : 13 + ups] = row_sum(cotangent_ref[...])
        vec_ref[11:12] = norm_back(
            x3_ref, 4, lambda span: cotangent_ref[span].astype(F32), dx, dx3_low
        )

        def branch(slot):
            def emit(r, result):
                dco[:, columns_of(r)] = result.astype(BF16)

            dot_tiles(dx3_low[...], weights, slot, emit, turned=True, unrolled=True)

        using(8, branch)

    def cross_back(first, last):
        def one(j, carry):
            columns = columns_of(j, LANES)
            dq, dk, dv = cross_grads(
                length_ref[0],
                cq_ref[:, columns],
                mem_ref[0, :, columns],
                mem_ref[1, :, columns],
                dco[:, columns],
                crossed_ref[:, columns],
                [cross_log_ref[j, h : h + 1] for h in range(LANES // HDIM)],
            )
            dcq[:, columns] = dq.astype(BF16)
            fill = jnp.zeros((max(padded - mem_rows, 1), LANES), F32)
            for peer in range(seqs):
                span = slice(peer * mem_rows, (peer + 1) * mem_rows)
                for part, values in enumerate((dk, dv)):
                    block = values[span]
                    if padded > mem_rows:
                        block = jnp.concatenate([block, fill], axis=0)
                    mem_parts[peer % 2, peer // 2, part, :, columns] = block.astype(BF16)
            return carry

        lax.fori_loop(first, last, one, 0)

    def memory_send():
        mem_fold().wait()

        def send(step):
            peer = lax.rem(chip + step, chips)
            mem_parts[place.core, peer] = mem_parts[place.core, peer] + mem_theirs[peer]

            @pl.when(step < chips)
            def _():
                mem_copy(peer, chip).start()

            @pl.when(step == chips)
            def _():
                mem_came[chip] = mem_parts[place.core, peer]

        loop(1, chips + 1, send)

    def do_copy(peer, slot):
        return remote(
            dq_low.at[peer], do_all.at[slot], do_send.at[peer], do_recv.at[slot], (peer, z)
        )

    def before_self():
        def inner(slot):
            def emit(r, result):
                dh[:, columns_of(r)] = result

            dot_tiles(dcq[...], weights, slot, emit, turned=True, unrolled=True)

        using(9, inner)
        vec_ref[9:10] = row_sum(dcq[...])
        vec_ref[8:9] = norm_back(x2_ref, 2, lambda span: dx[span], dx, dx2_low)

        def branch(slot):
            def emit(r, result):
                low = result.astype(BF16)
                for piece in range(tile // width):
                    dq_low[r * (tile // width) + piece] = low[
                        :, piece * width : (piece + 1) * width
                    ]

            dot_tiles(dx2_low[...], weights, slot, emit, turned=True, unrolled=True)

        using(10, branch)

        def send(step, carry):
            do_copy(lax.rem(me + step, seqs), me).start()
            return carry

        lax.fori_loop(1, seqs, send, 0)
        do_all[me] = dq_low[me]

    def memory_back():
        def arrive(step):
            peer = lax.rem(chip + step, chips)
            mem_copy(peer, peer).wait_recv()

        loop(1, chips, arrive)
        for part in range(2):
            part_sum = mem_came[0, part].astype(F32)
            for j in range(1, chips):
                part_sum = part_sum + mem_came[j, part].astype(F32)
            mem_low[part] = part_sum.astype(BF16)
        vec_ref[10:11] = row_sum(mem_low[1])

        def keys(slot):
            def emit(r, result):
                grad_memory_ref[:, columns_of(r)] = result

            dot_tiles(mem_low[0], weights, slot, emit, turned=True, unrolled=True)

        def values(slot):
            def emit(r, result):
                grad_memory_ref[:, columns_of(r)] = grad_memory_ref[:, columns_of(r)] + result

            dot_tiles(mem_low[1], weights, slot, emit, turned=True, unrolled=True)

        using(11, keys)
        using(12, values)

    window = window_ref[0]
    outputs = ((dq_low, dq_back), (dk_low, dk_back), (dv_low, dv_back))

    def returned(peer, slot, part):
        src, dst = outputs[part]
        return remote(
            src.at[peer],
            dst.at[:, pl.ds(pl.multiple_of(slot * width, width), width)],
            back_send.at[part, peer],
            back_recv.at[part, slot],
            (peer, z),
        )

    def prepare():
        def one(i, carry):
            @pl.when(i != me)
            def _():
                do_copy(i, i).wait_recv()

            sums = head_sums(do_all[i].astype(F32) * attended_ref[i].astype(F32), head_count)
            for head in range(head_count):
                delta[i, head : head + 1] = sums[head]
            for total in (dq_total, dk_total, dv_total):
                total[i] = jnp.zeros((rows, width), F32)
            return carry

        lax.fori_loop(0, seqs, one, 0)

    span_rows = 2 * rows
    stacked_queries = head_count * span_rows

    def tile_grads(p):
        level = (
            jnp.where(p >= 2, 1, 0) + jnp.where(p >= 6, 1, 0) + jnp.where(p >= 12, 1, 0)
        ).astype(jnp.int32)
        rank = p - level * (level + 1)
        second = jnp.where(rank > level, 1, 0).astype(jnp.int32)
        b = seqs - 1 - 2 * level - second
        q2 = seqs // 2 - 1 - level + rank - second * (level + 1)
        pair = pl.ds(pl.multiple_of(q2 * 2, 2), 2)
        keys, values = qkv_all[1, b], qkv_all[2, b]
        scaled = qkv_all[0, pair].reshape(span_rows, width) * jnp.asarray(HDIM**-0.5, BF16)
        grads = do_all[pair].reshape(span_rows, width)
        queries = jnp.concatenate([only_head(scaled, h, head_count) for h in range(head_count)], 0)
        uppers = jnp.concatenate([only_head(grads, h, head_count) for h in range(head_count)], 0)

        def row_of(ref):
            return jnp.concatenate(
                [ref[q2 * 2 + k, h : h + 1] for h in range(head_count) for k in range(2)], 1
            )

        logs, deltas = row_of(log_ref), row_of(delta)
        shape = (rows, stacked_queries)
        key_row = lax.broadcasted_iota(jnp.int32, shape, 0)
        query_row = lax.rem(lax.broadcasted_iota(jnp.int32, (1, stacked_queries), 1), span_rows)
        reach = query_row + (q2 * 2 - b) * rows

        def work(diagonal):
            scores = dot_nt(keys, queries)
            allowed = key_row <= reach if diagonal else key_row > reach - window
            probs = jnp.exp(jnp.where(allowed, scores, NEG_FILL) - logs)
            grad_scores = (probs * (dot_nt(values, uppers) - deltas)).astype(BF16)
            dv_total[b] = dv_total[b] + dot_nn(probs.astype(BF16), uppers)
            dk_total[b] = dk_total[b] + dot_nn(grad_scores, queries)
            spread = dot_tn(grad_scores, keys)
            part = spread[:span_rows]
            lane = lax.broadcasted_iota(jnp.int32, part.shape, 1)
            for h in range(1, head_count):
                part = jnp.where(
                    lane >= h * HDIM, spread[h * span_rows : (h + 1) * span_rows], part
                )
            dq_total[pair] = dq_total[pair] + part.reshape(2, rows, width)

        diagonal = lax.div(b, 2) == q2

        @pl.when(diagonal)
        def _():
            work(True)

        @pl.when(jnp.logical_not(diagonal))
        def _():
            work(False)

        @pl.when(q2 == seqs // 2 - 1)
        def _():
            dk_low[b] = dk_total[b].astype(BF16)
            dv_low[b] = dv_total[b].astype(BF16)
            send_back(b, 1)
            send_back(b, 2)

    def send_back(i, part):
        low, rows_ref = outputs[part]

        @pl.when(i != me)
        def _():
            returned(i, me, part).start()

        @pl.when(i == me)
        def _():
            rows_ref[:, pl.ds(pl.multiple_of(i * width, width), width)] = low[i]

    def close_self():
        loop(1, seqs, lambda step: do_copy(lax.rem(me + step, seqs), me).wait_send())

        def one(i):
            dq_low[i] = (dq_total[i] * HDIM**-0.5).astype(BF16)
            send_back(i, 0)

        loop(0, seqs, one)

    def first_arrive():
        def arrive(step, carry):
            peer = lax.rem(me + step, seqs)
            for part in range(3):
                returned(peer, peer, part).wait_recv()
            return carry

        lax.fori_loop(1, seqs, arrive, 0)

    def first_back():
        for part in range(3):

            def inner(slot, part=part):
                def emit(r, result):
                    if part == 0:
                        dh[:, columns_of(r)] = result
                    else:
                        dh[:, columns_of(r)] = dh[:, columns_of(r)] + result

                dot_tiles(rows_of_part[part][...], weights, slot, emit, turned=True, unrolled=True)

            using(13 + part, inner)
        vec_ref[6:7] = row_sum(rows_of_part[0][...])
        vec_ref[7:8] = row_sum(rows_of_part[2][...])
        norm_back(tokens_ref, 0, lambda span: dx[span], grad_tokens_ref, None)

    rows_of_part = (dq_back, dk_back, dv_back)

    def fold_copy(order):
        target = (place.sibling(), place.x_peer(), place.y_peer())[order]
        return remote(
            vec_part.at[order],
            vec_came.at[order],
            vec_send.at[order],
            vec_recv.at[order],
            target,
        )

    def across_copy(peer, slot):
        return remote(
            vec_planes.at[slot],
            vec_planes.at[slot],
            across_send.at[peer],
            across_recv.at[slot],
            (me, peer),
        )

    def fold_vectors(order):
        if order == 0:
            vec_part[0] = vec_ref[...]
        else:
            fold_copy(order - 1).wait()
            folded = vec_part[order - 1] + vec_came[order - 1]
            if order < 3:
                vec_part[order] = folded
            else:
                vec_planes[z] = folded
        if order < 3:
            fold_copy(order).start()
        else:

            def send(step, carry):
                across_copy(lax.rem(z + step, planes), z).start()
                return carry

            lax.fori_loop(1, planes, send, 0)

    def close_vectors():
        def arrive(step, carry):
            peer = lax.rem(z + step, planes)
            across_copy(peer, peer).wait()
            return carry

        lax.fori_loop(1, planes, arrive, 0)
        vector_sum = vec_planes[0]
        for plane in range(1, planes):
            vector_sum = vector_sum + vec_planes[plane]
        vec_sum_ref[...] = vector_sum

    slot_count = slots_ref.shape[0]

    def slot_copy(peer, holder, half):
        slot_rows, slot_columns = tile_of(holder, planes, half, slots_ref.shape[1])
        return remote(
            made.at[0, half, lax.div(peer, planes), lax.rem(peer, planes), pl.ds(0, slot_count)],
            slots_ref.at[:, slot_rows, slot_columns],
            slot_send.at[peer, half],
            slot_recv.at[holder, half],
            (lax.div(peer, planes), lax.rem(peer, planes)),
        )

    def return_tiles():
        def fill(peer):
            for s in range(slot_count):
                group, unit = group_ref[peer * slot_count + s], unit_ref[peer * slot_count + s]
                for half in range(2):
                    block = sums_ref[jnp.maximum(group, 0), half, unit]
                    made[0, half, lax.div(peer, planes), lax.rem(peer, planes), s] = jnp.where(
                        group >= 0, block, jnp.zeros_like(block)
                    )

        def start(step, carry):
            peer = lax.rem(here + step, total)
            fill(peer)
            for half in range(2):
                slot_copy(peer, here, half).start()
            return carry

        lax.fori_loop(1, total, start, 0)
        fill(here)
        own = []
        for half in range(2):
            slot_rows, slot_columns = tile_of(here, planes, half, slots_ref.shape[1])
            own.append(
                pltpu.make_async_copy(
                    made.at[0, half, lax.div(here, planes), lax.rem(here, planes), pl.ds(0, slot_count)],
                    slots_ref.at[:, slot_rows, slot_columns],
                    own_sem.at[half],
                )
            )
            own[half].start()
        for copy in own:
            copy.wait()

        def finish_slots(step, carry):
            peer = lax.rem(here + total - step, total)
            for half in range(2):
                slot_copy(peer, peer, half).wait()
            return carry

        lax.fori_loop(1, total, finish_slots, 0)

    def tick(t, carry):
        reduce.receive(t)

        slot = lax.rem(t, GRAD_SLOTS)

        @pl.when(t < ups)
        def _():
            grad_matrix(slot, act_ref, t * D, cotangent_ref)

        @pl.when((t >= ups) & (t < 2 * ups))
        def _():
            grad_matrix(slot, du, (t - ups) * D, h3_ref)

        late = 2 * ups
        pieces = (
            (crossed_ref, dx3_low),
            (h2_ref, dcq),
            (joined_ref, dx2_low),
            (memory_ref, mem_low.at[0]),
            (memory_ref, mem_low.at[1]),
        )
        for step, (left, right) in enumerate(pieces):

            @pl.when(t == late + step)
            def _(left=left, right=right):
                grad_matrix(slot, left, 0, right)

        last = late + len(pieces)

        @pl.when(t == last)
        def _():
            first_arrive()

        for part in range(3):

            @pl.when(t == last + part)
            def _(part=part):
                grad_matrix(slot, h1_ref, 0, rows_of_part[part])

        reduce.advance(t)

        def at(step, work):
            @pl.when(t == step)
            def _():
                work()

        for j in range(ups):
            at(1 + j // 2, functools.partial(hidden_back, j))
        at(3, cross_branch)
        blocks = D // LANES
        at(4, functools.partial(cross_back, 0, blocks // 2))
        at(5, functools.partial(cross_back, blocks // 2, blocks))
        at(5, lambda: mem_fold().start())
        at(6, memory_send)
        at(6, before_self)
        at(7, prepare)

        @pl.when((t >= 7) & (t < 13))
        def _():
            loop(lax.div(10 * (t - 7), 3), lax.div(10 * (t - 6), 3), tile_grads)

        at(10, memory_back)
        at(12, close_self)
        at(last + 3, first_back)
        for order in range(4):
            at(last + 4 + order, functools.partial(fold_vectors, order))
        at(last + 9, close_vectors)
        return carry

    lax.fori_loop(0, reduce.groups + reduce.last, tick, 0)

    def finish(step, carry):
        peer = lax.rem(me + step, seqs)
        for part in range(3):
            returned(peer, me, part).wait_send()
        return carry

    lax.fori_loop(1, seqs, finish, 0)
    loop(1, chips, lambda step: mem_copy(lax.rem(chip + step, chips), chip).wait_send())
    reduce.drain()
    return_tiles()


def backward_pass(seqs, planes, windows, lengths, group, unit, whole, slope, arrays):
    groups, matrix = whole.shape[0], whole.shape[1:]
    column = matrix[2:]
    block = matrix[3:]
    cotangent, memory = arrays[0], arrays[-2]
    total = seqs * planes
    slots, unit_rows = group.shape[0] // total, 2 * planes * block[1]
    rows = cotangent.shape[0]
    width = D // seqs
    padded = memory.shape[0]
    dma = pltpu.SemaphoreType.DMA
    vmem = pl.BlockSpec(memory_space=pltpu.VMEM)
    smem = pl.BlockSpec(memory_space=pltpu.SMEM)
    anywhere = pl.BlockSpec(memory_space=pl.ANY)
    shape = jax.ShapeDtypeStruct
    by_head = (seqs, rows, width)
    outs = pl.pallas_call(
        functools.partial(backward_kernel, seqs, planes),
        out_shape=(
            shape((groups, 2, 4) + column, BF16),
            shape((groups, 2, 2) + column, BF16),
            shape((groups, 2, planes - 1, 2, 2) + block, BF16),
            shape((slots, unit_rows, D), BF16),
            shape((rows, D), F32),
            shape((padded, D), F32),
            shape((24, D), F32),
        ),
        in_specs=[smem] * 4 + [anywhere, anywhere] + [vmem] * len(arrays),
        out_specs=(anywhere, anywhere, anywhere, anywhere, vmem, vmem, vmem),
        scratch_shapes=[
            pltpu.VMEM((groups, 2) + block, BF16),
            pltpu.VMEM((24, D), F32),
            pltpu.VMEM((3, 24, D), F32),
            pltpu.VMEM((3, 24, D), F32),
            pltpu.VMEM((planes, 24, D), F32),
            pltpu.VMEM((GRAD_SLOTS,) + matrix, BF16),
            pltpu.VMEM((2, 4) + column, BF16),
            pltpu.VMEM((2, 2) + column, BF16),
            pltpu.VMEM((groups, 2) + block, BF16),
            pltpu.VMEM((REDUCE_LIGHT, 2) + column, BF16),
            pltpu.VMEM((COLUMN_SLOTS, planes, 2, 2) + block, BF16),
            pltpu.VMEM((2, planes - 1, 2, 2) + block, BF16),
            pltpu.VMEM((2, planes - 1, 2) + block, BF16),
            pltpu.VMEM((READ_SLOTS,) + matrix, BF16),
            pltpu.VMEM((rows, D), F32),
            pltpu.VMEM((rows, D), F32),
            pltpu.VMEM((rows, FF), BF16),
            pltpu.VMEM((rows, D), BF16),
            pltpu.VMEM((rows, D), BF16),
            pltpu.VMEM((rows, D), BF16),
            pltpu.VMEM((rows, D), BF16),
            pltpu.VMEM((2, seqs // 2, 2, padded, D), BF16),
            pltpu.VMEM((seqs // 2, 2, padded, D), BF16),
            pltpu.VMEM((seqs // 2, 2, padded, D), BF16),
            pltpu.VMEM((2, padded, D), BF16),
            pltpu.VMEM(by_head, BF16),
            pltpu.VMEM((seqs, 8, rows), F32),
            pltpu.VMEM(by_head, F32),
            pltpu.VMEM(by_head, F32),
            pltpu.VMEM(by_head, F32),
            pltpu.VMEM(by_head, BF16),
            pltpu.VMEM(by_head, BF16),
            pltpu.VMEM(by_head, BF16),
            pltpu.VMEM((rows, D), BF16),
            pltpu.VMEM((rows, D), BF16),
            pltpu.VMEM((rows, D), BF16),
            dma((2,)),
            dma((2, 2, planes - 1)),
            dma((groups,)),
            dma((groups,)),
            dma((groups, 2, 2)),
            dma((groups, 2, 2)),
            dma((groups, 2, planes - 1)),
            dma((groups, 2, planes - 1)),
            dma((READ_SLOTS,)),
            dma(()),
            dma(()),
            dma(()),
            dma((seqs // 2,)),
            dma((seqs // 2,)),
            dma((seqs,)),
            dma((seqs,)),
            dma((3, seqs)),
            dma((3, seqs)),
            dma((3,)),
            dma((3,)),
            dma((planes,)),
            dma((planes,)),
            dma((total, 2)),
            dma((total, 2)),
            dma((2,)),
        ],
        compiler_params=pltpu.CompilerParams(
            collective_id=3, has_side_effects=True, vmem_limit_bytes=60 * MIB
        ),
        name="backward_pass",
    )(windows, lengths, group, unit, whole, slope, *arrays)
    return outs[3:]


def dot_nt(left, right):
    return lax.dot_general(left, right, (((1,), (1,)), ((), ())), preferred_element_type=F32)


def dot_tn(left, right):
    return lax.dot_general(left, right, (((0,), (0,)), ((), ())), preferred_element_type=F32)


def dot_nn(left, right):
    return lax.dot_general(left, right, (((1,), (0,)), ((), ())), preferred_element_type=F32)


def only_head(values, head, head_count):
    if head_count == 1:
        return values
    lane = lax.broadcasted_iota(jnp.int32, values.shape, 1)
    inside = (lane >= head * HDIM) & (lane < (head + 1) * HDIM)
    return jnp.where(inside, values, jnp.zeros_like(values))


def stacked_heads(parts):
    whole = parts[0]
    row = lax.broadcasted_iota(jnp.int32, whole.shape, 0)
    for head in range(1, len(parts)):
        whole = jnp.where(row >= head * HDIM, parts[head], whole)
    return whole


def head_sums(values, head_count):
    turned = values.T
    return [
        jnp.sum(turned[head * HDIM : (head + 1) * HDIM], axis=0, keepdims=True)
        for head in range(head_count)
    ]


def attend_block(i, rows, head_count, offset, window, q_all, k_all, v_all, log_ref):
    scaled = q_all[i] * jnp.asarray(HDIM**-0.5, BF16)
    queries = [only_head(scaled, head, head_count) for head in range(head_count)]
    state = []
    for head in range(head_count):
        scores = dot_nt(k_all[i], queries[head])
        scores = jnp.where((offset <= 0) & (offset > -window), scores, NEG_FILL)
        best = jnp.max(scores, axis=0, keepdims=True)
        probs = jnp.exp(scores - best)
        state.append(
            (best, jnp.sum(probs, axis=0, keepdims=True), dot_tn(v_all[i], probs.astype(BF16)))
        )

    def key_block(b, running):
        keys, values = k_all[b], v_all[b]
        limit = (i - b) * rows - window
        renewed = []
        for head in range(head_count):
            best, total, gathered = running[head]
            scores = jnp.where(offset > limit, dot_nt(keys, queries[head]), NEG_FILL)
            new_best = jnp.maximum(best, jnp.max(scores, axis=0, keepdims=True))
            probs = jnp.exp(scores - new_best)
            keep = jnp.exp(best - new_best)
            renewed.append(
                (
                    new_best,
                    total * keep + jnp.sum(probs, axis=0, keepdims=True),
                    gathered * keep + dot_tn(values, probs.astype(BF16)),
                )
            )
        return tuple(renewed)

    state = lax.fori_loop(0, i, key_block, tuple(state))
    for head in range(head_count):
        best, total, _ = state[head]
        log_ref[i, head : head + 1] = best + jnp.log(total)
    return stacked_heads([gathered / total for _, total, gathered in state]).T


def attend_pairs(i, rows, head_count, window, qkv_all, log_ref):
    width = qkv_all.shape[3]
    scaled = qkv_all[0, i] * jnp.asarray(HDIM**-0.5, BF16)
    queries = jnp.concatenate([only_head(scaled, head, head_count) for head in range(head_count)], 0)
    columns = head_count * rows
    key_row = lax.broadcasted_iota(jnp.int32, (2 * rows, columns), 0)
    query_row = lax.rem(lax.broadcasted_iota(jnp.int32, (1, columns), 1), rows)
    last = lax.div(i, 2)

    def two_blocks(part, m):
        return qkv_all[part, pl.ds(pl.multiple_of(2 * m, 2), 2)].reshape(2 * rows, width)

    def one(step, running):
        m = last - step
        best, total, gathered = running
        reach = query_row + (i - 2 * m) * rows
        allowed = (key_row <= reach) & (key_row > reach - window)
        scores = jnp.where(allowed, dot_nt(two_blocks(1, m), queries), NEG_FILL)
        new_best = jnp.maximum(best, jnp.max(scores, axis=0, keepdims=True))
        probs = jnp.exp(scores - new_best)
        keep = jnp.exp(best - new_best)
        return (
            new_best,
            total * keep + jnp.sum(probs, axis=0, keepdims=True),
            gathered * keep + dot_tn(two_blocks(2, m), probs.astype(BF16)),
        )

    best, total, gathered = lax.fori_loop(
        0,
        last + 1,
        one,
        (
            jnp.full((1, columns), NEG_FILL, F32),
            jnp.zeros((1, columns), F32),
            jnp.zeros((width, columns), F32),
        ),
    )
    logs = best + jnp.log(total)
    gathered = gathered / total
    for head in range(head_count):
        log_ref[i, head : head + 1] = logs[:, head * rows : (head + 1) * rows]
    return stacked_heads(
        [gathered[:, head * rows : (head + 1) * rows] for head in range(head_count)]
    ).T


def cross_attend(length, query, keys, values):
    head_count = LANES // HDIM
    rows = query.shape[0]
    scaled = query * jnp.asarray(HDIM**-0.5, BF16)
    queries = jnp.concatenate([only_head(scaled, head, head_count) for head in range(head_count)], 0)
    scores = dot_nt(keys, queries)
    allowed = lax.broadcasted_iota(jnp.int32, scores.shape, 0) < length
    scores = jnp.where(allowed, scores, NEG_FILL)
    best = jnp.max(scores, axis=0, keepdims=True)
    probs = jnp.exp(scores - best)
    total = jnp.sum(probs, axis=0, keepdims=True)
    gathered = dot_tn(values, probs.astype(BF16)) / total
    logs = best + jnp.log(total)
    spans = [slice(head * rows, (head + 1) * rows) for head in range(head_count)]
    crossed = stacked_heads([gathered[:, span] for span in spans]).T
    return crossed, [logs[:, span] for span in spans]


def self_forward_kernel(
    seqs,
    window_ref,
    q_ref,
    k_ref,
    v_ref,
    joined_ref,
    q_all,
    k_all,
    v_all,
    attended_ref,
    log_ref,
    rounded,
    send_sem,
    recv_sem,
    back_send,
    back_recv,
):
    me, z = lax.axis_index("seq"), lax.axis_index("grp")
    rows, width = q_ref.shape[1], q_ref.shape[2]
    head_count = width // HDIM
    greet_all(me, seqs, lambda j: (j, z))
    pairs = ((q_ref, q_all), (k_ref, k_all), (v_ref, v_all))

    def outward(peer, slot, part):
        src, dst = pairs[part]
        return remote(
            src.at[peer], dst.at[slot], send_sem.at[part, peer], recv_sem.at[part, slot], (peer, z)
        )

    def start(step, carry):
        peer = lax.rem(me + step, seqs)
        for part in range(3):
            outward(peer, me, part).start()
        return carry

    lax.fori_loop(1, seqs, start, 0)
    for src, dst in pairs:
        dst[me] = src[me]
    window = window_ref[0]
    offset = lax.broadcasted_iota(jnp.int32, (rows, rows), 0) - lax.broadcasted_iota(
        jnp.int32, (rows, rows), 1
    )

    def backward_copy(peer, slot):
        return remote(
            rounded.at[peer], joined_ref.at[slot], back_send.at[peer], back_recv.at[slot], (peer, z)
        )

    def query_block(i, carry):
        @pl.when(i != me)
        def _():
            for part in range(3):
                outward(i, i, part).wait_recv()

        attended = attend_block(i, rows, head_count, offset, window, q_all, k_all, v_all, log_ref)
        attended_ref[i] = attended
        rounded[i] = attended.astype(BF16)

        @pl.when(i != me)
        def _():
            backward_copy(i, me).start()

        @pl.when(i == me)
        def _():
            joined_ref[i] = rounded[i]

        return carry

    lax.fori_loop(0, seqs, query_block, 0)

    def finish(step, carry):
        peer = lax.rem(me + step, seqs)
        for part in range(3):
            outward(peer, me, part).wait_send()
        backward_copy(peer, peer).wait()
        return carry

    lax.fori_loop(1, seqs, finish, 0)


def self_forward(seqs, windows, query, key, value):
    shape = query.shape
    head_count = shape[2] // HDIM
    dma = pltpu.SemaphoreType.DMA
    vmem = pl.BlockSpec(memory_space=pltpu.VMEM)
    return pl.pallas_call(
        functools.partial(self_forward_kernel, seqs),
        out_shape=(
            jax.ShapeDtypeStruct(shape, BF16),
            jax.ShapeDtypeStruct(shape, BF16),
            jax.ShapeDtypeStruct(shape, BF16),
            jax.ShapeDtypeStruct(shape, BF16),
            jax.ShapeDtypeStruct(shape, F32),
            jax.ShapeDtypeStruct((seqs, max(head_count, 8), shape[1]), F32),
        ),
        in_specs=[pl.BlockSpec(memory_space=pltpu.SMEM), vmem, vmem, vmem],
        out_specs=(vmem,) * 6,
        scratch_shapes=[
            pltpu.VMEM(shape, BF16),
            dma((3, seqs)),
            dma((3, seqs)),
            dma((seqs,)),
            dma((seqs,)),
        ],
        compiler_params=pltpu.CompilerParams(
            collective_id=5, has_side_effects=True, vmem_limit_bytes=40 * MIB
        ),
        name="self_forward",
    )(windows, query, key, value)


def key_grads(
    b, seqs, rows, head_count, offset, window,
    q_all, k_all, v_all, grad_all, log_ref, delta, dq_total,
):
    keys, values = k_all[b], v_all[b]
    width = keys.shape[1]
    scale = jnp.asarray(HDIM**-0.5, BF16)
    key_heads = [only_head(keys, head, head_count) for head in range(head_count)]

    def pair(i, sums, diagonal):
        dk, dv = sums
        scaled = q_all[i] * scale
        grads = grad_all[i]
        if diagonal:
            allowed = (offset <= 0) & (offset > -window)
        else:
            allowed = offset > (i - b) * rows - window
        dq = dq_total[i]
        for head in range(head_count):
            query = only_head(scaled, head, head_count)
            grad = only_head(grads, head, head_count)
            scores = jnp.where(allowed, dot_nt(keys, query), NEG_FILL)
            probs = jnp.exp(scores - log_ref[i, head : head + 1])
            spread = dot_nt(values, grad)
            grad_scores = (probs * (spread - delta[i, head : head + 1])).astype(BF16)
            dv = dv + dot_nn(probs.astype(BF16), grad)
            dk = dk + dot_nn(grad_scores, query)
            dq = dq + dot_tn(grad_scores, key_heads[head])
        dq_total[i] = dq
        return (dk, dv)

    zeros = jnp.zeros((rows, width), F32)
    sums = pair(b, (zeros, zeros), True)
    return lax.fori_loop(b + 1, seqs, lambda i, s: pair(i, s, False), sums)


def cross_grads(length, query, keys, values, grads, crossed, logs):
    head_count = LANES // HDIM
    rows = query.shape[0]
    scaled = query * jnp.asarray(HDIM**-0.5, BF16)
    queries = jnp.concatenate([only_head(scaled, head, head_count) for head in range(head_count)], 0)
    uppers = jnp.concatenate([only_head(grads, head, head_count) for head in range(head_count)], 0)
    deltas = jnp.concatenate(head_sums(grads.astype(F32) * crossed.astype(F32), head_count), 1)
    scores = dot_nt(keys, queries)
    allowed = lax.broadcasted_iota(jnp.int32, scores.shape, 0) < length
    probs = jnp.exp(jnp.where(allowed, scores, NEG_FILL) - jnp.concatenate(logs, 1))
    grad_scores = (probs * (dot_nt(values, uppers) - deltas)).astype(BF16)
    dv = dot_nn(probs.astype(BF16), uppers)
    dk = dot_nn(grad_scores, queries)
    spread = dot_tn(grad_scores, keys)
    dq = spread[:rows]
    lane = lax.broadcasted_iota(jnp.int32, dq.shape, 1)
    for head in range(1, head_count):
        dq = jnp.where(lane >= head * HDIM, spread[head * rows : (head + 1) * rows], dq)
    return dq * HDIM**-0.5, dk, dv


def self_backward_kernel(
    seqs,
    window_ref,
    grad_ref,
    q_all,
    k_all,
    v_all,
    attended_ref,
    log_ref,
    dq_ref,
    dk_ref,
    dv_ref,
    grad_all,
    delta,
    dq_total,
    dq_low,
    dk_low,
    dv_low,
    send_sem,
    recv_sem,
    back_send,
    back_recv,
):
    me, z = lax.axis_index("seq"), lax.axis_index("grp")
    rows, width = grad_ref.shape[1], grad_ref.shape[2]
    head_count = width // HDIM
    greet_all(me, seqs, lambda j: (j, z))

    def outward(peer, slot):
        return remote(
            grad_ref.at[peer], grad_all.at[slot], send_sem.at[peer], recv_sem.at[slot], (peer, z)
        )

    def start(step, carry):
        outward(lax.rem(me + step, seqs), me).start()
        return carry

    lax.fori_loop(1, seqs, start, 0)
    grad_all[me] = grad_ref[me]
    window = window_ref[0]
    offset = lax.broadcasted_iota(jnp.int32, (rows, rows), 0) - lax.broadcasted_iota(
        jnp.int32, (rows, rows), 1
    )

    def prepare(i, carry):
        @pl.when(i != me)
        def _():
            outward(i, i).wait_recv()

        sums = head_sums(grad_all[i].astype(F32) * attended_ref[i].astype(F32), head_count)
        for head in range(head_count):
            delta[i, head : head + 1] = sums[head]
        dq_total[i] = jnp.zeros((rows, width), F32)
        return carry

    lax.fori_loop(0, seqs, prepare, 0)
    outputs = ((dq_low, dq_ref), (dk_low, dk_ref), (dv_low, dv_ref))

    def returned(peer, slot, part):
        src, dst = outputs[part]
        return remote(
            src.at[peer], dst.at[slot], back_send.at[part, peer], back_recv.at[part, slot], (peer, z)
        )

    def key_block(step, carry):
        b = seqs - 1 - step
        dk, dv = key_grads(
            b, seqs, rows, head_count, offset, window,
            q_all, k_all, v_all, grad_all, log_ref, delta, dq_total,
        )
        dk_low[b] = dk.astype(BF16)
        dv_low[b] = dv.astype(BF16)

        @pl.when(b != me)
        def _():
            returned(b, me, 1).start()
            returned(b, me, 2).start()

        return carry

    lax.fori_loop(0, seqs, key_block, 0)

    def close(i, carry):
        dq_low[i] = (dq_total[i] * HDIM**-0.5).astype(BF16)

        @pl.when(i != me)
        def _():
            returned(i, me, 0).start()

        return carry

    lax.fori_loop(0, seqs, close, 0)
    for src, dst in outputs:
        dst[me] = src[me]

    def finish(step, carry):
        peer = lax.rem(me + step, seqs)
        outward(peer, me).wait_send()
        for part in range(3):
            returned(peer, peer, part).wait()
        return carry

    lax.fori_loop(1, seqs, finish, 0)


def self_backward(seqs, windows, grad, query_all, key_all, value_all, attended, logs):
    shape = grad.shape
    dma = pltpu.SemaphoreType.DMA
    vmem = pl.BlockSpec(memory_space=pltpu.VMEM)
    return pl.pallas_call(
        functools.partial(self_backward_kernel, seqs),
        out_shape=(jax.ShapeDtypeStruct(shape, BF16),) * 3,
        in_specs=[pl.BlockSpec(memory_space=pltpu.SMEM)] + [vmem] * 6,
        out_specs=(vmem,) * 3,
        scratch_shapes=[
            pltpu.VMEM(shape, BF16),
            pltpu.VMEM(logs.shape, F32),
            pltpu.VMEM(shape, F32),
            pltpu.VMEM(shape, BF16),
            pltpu.VMEM(shape, BF16),
            pltpu.VMEM(shape, BF16),
            dma((seqs,)),
            dma((seqs,)),
            dma((3, seqs)),
            dma((3, seqs)),
        ],
        compiler_params=pltpu.CompilerParams(
            collective_id=6, has_side_effects=True, vmem_limit_bytes=40 * MIB
        ),
        name="self_backward",
    )(windows, grad, query_all, key_all, value_all, attended, logs)


def cross_forward_kernel(length_ref, q_ref, k_ref, v_ref, crossed_ref, low_ref, log_ref):
    crossed, logs = cross_attend(length_ref[0], q_ref[...], k_ref[...], v_ref[...])
    for head in range(len(logs)):
        log_ref[0, head : head + 1] = logs[head]
    crossed_ref[...] = crossed
    low_ref[...] = crossed.astype(BF16)


def cross_forward(lengths, query, key, value):
    rows, width = query.shape
    blocks = width // LANES
    columns = lambda j: (0, j)
    return pl.pallas_call(
        cross_forward_kernel,
        grid=(blocks,),
        out_shape=(
            jax.ShapeDtypeStruct((rows, width), F32),
            jax.ShapeDtypeStruct((rows, width), BF16),
            jax.ShapeDtypeStruct((blocks, 8, rows), F32),
        ),
        in_specs=[
            pl.BlockSpec(memory_space=pltpu.SMEM),
            pl.BlockSpec((rows, LANES), columns),
            pl.BlockSpec((key.shape[0], LANES), columns),
            pl.BlockSpec((key.shape[0], LANES), columns),
        ],
        out_specs=(
            pl.BlockSpec((rows, LANES), columns),
            pl.BlockSpec((rows, LANES), columns),
            pl.BlockSpec((1, 8, rows), lambda j: (j, 0, 0)),
        ),
        name="cross_forward",
    )(lengths, query, key, value)


def cross_backward_kernel(
    length_ref, q_ref, k_ref, v_ref, grad_ref, crossed_ref, log_ref, dq_ref, dk_ref, dv_ref
):
    dq, dk, dv = cross_grads(
        length_ref[0],
        q_ref[...],
        k_ref[...],
        v_ref[...],
        grad_ref[...],
        crossed_ref[...],
        [log_ref[0, head : head + 1] for head in range(LANES // HDIM)],
    )
    dq_ref[...] = dq.astype(BF16)
    dk_ref[...] = dk.astype(BF16)
    dv_ref[...] = dv.astype(BF16)


def cross_backward(lengths, query, key, value, grad, crossed, logs):
    rows, width = query.shape
    keys = key.shape[0]
    columns = lambda j: (0, j)
    token_block = pl.BlockSpec((rows, LANES), columns)
    key_block = pl.BlockSpec((keys, LANES), columns)
    return pl.pallas_call(
        cross_backward_kernel,
        grid=(width // LANES,),
        out_shape=(
            jax.ShapeDtypeStruct((rows, width), BF16),
            jax.ShapeDtypeStruct((keys, width), BF16),
            jax.ShapeDtypeStruct((keys, width), BF16),
        ),
        in_specs=[
            pl.BlockSpec(memory_space=pltpu.SMEM),
            token_block,
            key_block,
            key_block,
            token_block,
            token_block,
            pl.BlockSpec((1, 8, rows), lambda j: (j, 0, 0)),
        ],
        out_specs=(token_block, key_block, key_block),
        name="cross_backward",
    )(lengths, query, key, value, grad, crossed, logs)


def memory_sum_kernel(seqs, parts_ref, total_ref, arrived, send_sem, recv_sem):
    me, z = lax.axis_index("seq"), lax.axis_index("grp")
    greet_all(me, seqs, lambda j: (j, z))

    def copy_of(peer, slot):
        return remote(
            parts_ref.at[peer], arrived.at[slot], send_sem.at[peer], recv_sem.at[slot], (peer, z)
        )

    def start(step, carry):
        copy_of(lax.rem(me + step, seqs), me).start()
        return carry

    def finish(step, carry):
        peer = lax.rem(me + step, seqs)
        copy_of(peer, peer).wait()
        return carry

    lax.fori_loop(1, seqs, start, 0)
    arrived[me] = parts_ref[me]
    lax.fori_loop(1, seqs, finish, 0)
    total = arrived[0].astype(F32)
    for j in range(1, seqs):
        total = total + arrived[j].astype(F32)
    total_ref[...] = total.astype(BF16)


def memory_sum(seqs, parts):
    dma = pltpu.SemaphoreType.DMA
    vmem = pl.BlockSpec(memory_space=pltpu.VMEM)
    return pl.pallas_call(
        functools.partial(memory_sum_kernel, seqs),
        out_shape=jax.ShapeDtypeStruct(parts.shape[1:], BF16),
        in_specs=[vmem],
        out_specs=vmem,
        scratch_shapes=[pltpu.VMEM(parts.shape, BF16), dma((seqs,)), dma((seqs,))],
        compiler_params=pltpu.CompilerParams(
            collective_id=7, has_side_effects=True, vmem_limit_bytes=32 * MIB
        ),
        name="memory_sum",
    )(parts)


def tiled_layer(
    tokens, memory, cotangent, windows, mem_lengths, owners, master, vectors
):
    rows = tokens.shape[1]
    mem_rows = memory.shape[1]
    seqs, planes = lax.axis_size("seq"), lax.axis_size("grp")
    holder, slot, group, unit = owner_tables(owners, master.shape[0], seqs * planes)
    memory_padded = jnp.pad(memory.reshape(mem_rows, D), ((0, -mem_rows % 16), (0, 0)))
    flat = tokens.reshape(rows, D)
    (
        whole,
        h1,
        joined,
        qkv,
        attended,
        logs,
        x2,
        h2,
        cross_queries,
        mem_acts,
        crossed,
        cross_logs,
        x3,
        h3,
        activation,
        slope,
        mixed,
    ) = forward_pass(
        seqs,
        planes,
        windows,
        mem_lengths,
        holder,
        slot,
        master,
        flat,
        memory_padded,
        seqs * mem_rows,
        vectors,
    )
    grad_slots, grad_tokens, grad_memory, vector_sums = backward_pass(
        seqs,
        planes,
        windows,
        mem_lengths,
        group,
        unit,
        whole,
        slope,
        (
            cotangent.reshape(rows, D),
            flat,
            x2,
            x3,
            h1,
            h2,
            h3,
            activation,
            crossed,
            cross_queries,
            mem_acts,
            cross_logs,
            joined,
            attended,
            qkv,
            logs,
            memory_padded,
            vectors,
        ),
    )
    return (
        mixed.reshape(tokens.shape),
        grad_tokens.reshape(tokens.shape),
        grad_memory[:mem_rows].reshape(memory.shape),
        grad_slots,
        vector_sums[: vectors.shape[0]],
    )


def plain_layer(
    tokens, memory, cotangent, windows, mem_lengths, owners, master, vectors
):
    rows = tokens.shape[1]
    seqs, planes = lax.axis_size("seq"), lax.axis_size("grp")
    units = owners.shape[0]
    slot_count, unit_rows = (master.shape[0], master.shape[1])
    bias_rows = FF // D
    placed, unit_at, occupied = slot_tables(owners, slot_count, seqs * planes)
    gathered = lax.all_gather(master.astype(BF16), ("seq", "grp"), axis=0, tiled=True)
    stacked = jnp.take(gathered, placed, axis=0).reshape(-1, D)
    memory_whole = lax.all_gather(memory[0], "seq", axis=0, tiled=True)
    self_query, self_key, self_value, self_out = (stacked[i * D : (i + 1) * D] for i in range(4))
    cross_query, cross_key, cross_value, cross_out = (
        stacked[i * D : (i + 1) * D] for i in range(4, 8)
    )
    hidden_in, hidden_out = stacked[8 * D : 8 * D + FF], stacked[8 * D + FF :]

    def by_device(tensor):
        return jnp.swapaxes(tensor.reshape(rows, seqs, D // seqs), 0, 1)

    def by_token(tensor):
        return jnp.swapaxes(tensor, 0, 1).reshape(rows, D)

    stream = tokens.astype(F32).reshape(rows, D)
    normed_one, form_one, inverse_one = norm_forward(stream, vectors[0], vectors[1])
    normed_self = normed_one.astype(BF16)
    query_act = (product(normed_self, self_query) + vectors[6]).astype(BF16)
    key_act = product(normed_self, self_key).astype(BF16)
    value_act = (product(normed_self, self_value) + vectors[7]).astype(BF16)
    joined, query_all, key_all, value_all, attended32, logs = self_forward(
        seqs, windows, by_device(query_act), by_device(key_act), by_device(value_act)
    )
    attended = by_token(joined)
    after_self = stream + product(attended, self_out) + vectors[8]
    normed_two, form_two, inverse_two = norm_forward(after_self, vectors[2], vectors[3])
    normed_cross = normed_two.astype(BF16)
    cross_queries = (product(normed_cross, cross_query) + vectors[9]).astype(BF16)
    mem_key_act = product(memory_whole, cross_key).astype(BF16)
    mem_value_act = (product(memory_whole, cross_value) + vectors[10]).astype(BF16)
    crossed32, crossed, cross_logs = cross_forward(
        mem_lengths, cross_queries, mem_key_act, mem_value_act
    )
    after_cross = after_self + product(crossed, cross_out) + vectors[11]
    normed_three, form_three, inverse_three = norm_forward(after_cross, vectors[4], vectors[5])
    normed_mlp = normed_three.astype(BF16)
    pre_act = product_nt(normed_mlp, hidden_in) + vectors[12 : 12 + bias_rows].reshape(FF)
    activation, slope = jax.jvp(gelu_exact, (pre_act,), (jnp.ones_like(pre_act),))
    activation_bf = activation.astype(BF16)
    result_rows = after_cross + product(activation_bf, hidden_out) + vectors[12 + bias_rows]
    mixed = result_rows.astype(BF16).reshape(tokens.shape)
    grad_out_bf = cotangent.reshape(rows, D)
    grad_stream = cotangent.astype(F32).reshape(rows, D)
    grad_hidden_out = product_tn(activation_bf, grad_out_bf)
    grad_down_bias = jnp.sum(grad_stream, axis=0)
    grad_activation = product_nt(grad_out_bf, hidden_out)
    grad_pre = (grad_activation * slope).astype(BF16)
    grad_hidden_in = product_tn(grad_pre, normed_mlp)
    grad_up_bias = jnp.sum(grad_pre.astype(F32), axis=0)
    grad_normed_mlp = product(grad_pre, hidden_in)
    back_three, grad_gain_three, grad_shift_three = norm_backward(
        grad_normed_mlp, form_three, inverse_three, vectors[4]
    )
    grad_after_cross = grad_stream + back_three
    grad_cross_branch = grad_after_cross.astype(BF16)
    grad_cross_out = product_tn(crossed, grad_cross_branch)
    grad_cross_out_bias = jnp.sum(grad_cross_branch.astype(F32), axis=0)
    grad_crossed = product_nt(grad_cross_branch, cross_out).astype(BF16)
    grad_cross_queries, part_mem_keys, part_mem_values = cross_backward(
        mem_lengths, cross_queries, mem_key_act, mem_value_act, grad_crossed, crossed32, cross_logs
    )
    mem_rows = memory.shape[1]
    mem_parts = jnp.concatenate(
        [part_mem_keys.reshape(seqs, mem_rows, D), part_mem_values.reshape(seqs, mem_rows, D)],
        axis=1,
    )
    mem_sums = memory_sum(seqs, mem_parts)
    mem_flat = memory.reshape(-1, D)
    mem_keys_flat = mem_sums[:mem_rows]
    mem_values_flat = mem_sums[mem_rows:]
    grad_cross_key = product_tn(mem_flat, mem_keys_flat)
    grad_cross_value = product_tn(mem_flat, mem_values_flat)
    grad_cross_value_bias = jnp.sum(mem_values_flat.astype(F32), axis=0)
    grad_memory = (
        product_nt(mem_keys_flat, cross_key) + product_nt(mem_values_flat, cross_value)
    ).reshape(memory.shape)
    grad_cross_query = product_tn(normed_cross, grad_cross_queries)
    grad_cross_query_bias = jnp.sum(grad_cross_queries.astype(F32), axis=0)
    grad_normed_cross = product_nt(grad_cross_queries, cross_query)
    back_two, grad_gain_two, grad_shift_two = norm_backward(
        grad_normed_cross, form_two, inverse_two, vectors[2]
    )
    grad_after_self = grad_after_cross + back_two
    grad_self_branch = grad_after_self.astype(BF16)
    grad_self_out = product_tn(attended, grad_self_branch)
    grad_self_out_bias = jnp.sum(grad_self_branch.astype(F32), axis=0)
    grad_attended = product_nt(grad_self_branch, self_out).astype(BF16)
    grad_queries, grad_keys, grad_values = (
        by_token(part)
        for part in self_backward(
            seqs, windows, by_device(grad_attended), query_all, key_all, value_all, attended32, logs
        )
    )
    grad_self_query = product_tn(normed_self, grad_queries)
    grad_self_key = product_tn(normed_self, grad_keys)
    grad_self_value = product_tn(normed_self, grad_values)
    grad_query_bias = jnp.sum(grad_queries.astype(F32), axis=0)
    grad_value_bias = jnp.sum(grad_values.astype(F32), axis=0)
    grad_normed_self = (
        product_nt(grad_queries, self_query)
        + product_nt(grad_keys, self_key)
        + product_nt(grad_values, self_value)
    )
    back_one, grad_gain_one, grad_shift_one = norm_backward(
        grad_normed_self, form_one, inverse_one, vectors[0]
    )
    grad_tokens = (grad_after_self + back_one).reshape(tokens.shape)
    grad_matrices = jnp.concatenate(
        [
            part.astype(BF16)
            for part in (
                grad_self_query,
                grad_self_key,
                grad_self_value,
                grad_self_out,
                grad_cross_query,
                grad_cross_key,
                grad_cross_value,
                grad_cross_out,
                grad_hidden_in,
                grad_hidden_out,
            )
        ],
        axis=0,
    )
    grad_units = grad_matrices.reshape(units, unit_rows, D)
    small_rows = jnp.stack(
        [
            grad_gain_one,
            grad_shift_one,
            grad_gain_two,
            grad_shift_two,
            grad_gain_three,
            grad_shift_three,
            grad_query_bias,
            grad_value_bias,
            grad_self_out_bias,
            grad_cross_query_bias,
            grad_cross_value_bias,
            grad_cross_out_bias,
        ]
    )
    grad_vectors = jnp.concatenate(
        [small_rows, grad_up_bias.reshape(bias_rows, D), grad_down_bias[None]], axis=0
    )
    grad_slots = lax.psum_scatter(
        jnp.where(
            occupied[:, None, None], jnp.take(grad_units, unit_at, axis=0), jnp.zeros((), BF16)
        ),
        ("seq", "grp"),
        scatter_dimension=0,
        tiled=True,
    )
    grad_vectors = lax.psum(grad_vectors, ("seq", "grp"))
    return mixed, grad_tokens, grad_memory, grad_slots, grad_vectors


def local(
    tokens,
    memory,
    cotangent,
    windows,
    mem_lengths,
    owners,
    master,
    first_moment,
    second_moment,
    vectors,
    vec_first,
    vec_second,
):
    tiled = lax.axis_size("seq") == 8 and master.shape[1] % (32 * lax.axis_size("grp")) == 0
    layer = tiled_layer if tiled else plain_layer
    mixed, grad_tokens, grad_memory, grad_slots, grad_vectors = layer(
        tokens, memory, cotangent, windows, mem_lengths, owners, master, vectors
    )
    grad_slots = grad_slots.astype(F32)
    new_first, new_second, new_master = adam_step(
        master, first_moment, second_moment, grad_slots, RATE_MATRIX, WEIGHT_DECAY
    )
    master_copy = new_master.astype(BF16)
    vec_first_out, vec_second_out, vectors_out = adam_step(
        vectors, vec_first, vec_second, grad_vectors, RATE_VECTOR, 0.0
    )
    grad_out_bias = grad_vectors[vectors.shape[0] - 1]
    return (
        mixed,
        grad_tokens,
        grad_memory,
        new_first,
        new_second,
        new_master,
        master_copy,
        vec_first_out,
        vec_second_out,
        vectors_out,
        grad_out_bias,
    )


def solution(mesh):
    placed = (
        P("grp", "seq", None),
        P("grp", "seq", None),
        P("grp", "seq", None),
        P("grp"),
        P("grp"),
        P(),
        P(("seq", "grp"), None, None),
        P(("seq", "grp"), None, None),
        P(("seq", "grp"), None, None),
        P(),
        P(),
        P(),
    )
    return jax.shard_map(
        local,
        mesh=mesh,
        in_specs=placed,
        out_specs=(
            P("grp", "seq", None),
            P("grp", "seq", None),
            P("grp", "seq", None),
            P(("seq", "grp"), None, None),
            P(("seq", "grp"), None, None),
            P(("seq", "grp"), None, None),
            P(("seq", "grp"), None, None),
            P(),
            P(),
            P(),
            P(),
        ),
        check_vma=False,
    )
```

time: 1950 us -> 471 us (0.24)
  waiting for transfers between devices: 1190 us -> 0 us
  Pallas kernels: 0 us -> 452 us
  matrix products: 200 us -> 0 us
  local copies, waits for them, and re-layouts: 194 us -> 6.28 us
  other arithmetic: 187 us -> 9.3 us
  starting transfers between devices: 131 us -> 0 us
    reduce_scatter x1 -> x0, waiting for transfers between devices: 808 us -> none  [local(): lax.psum_scatter(jnp.where(occupied[:, None, None], jnp.take(grad_units,...]
    pallas_call x0 -> x3, Pallas kernels: none -> 452 us  [the longest x1 241 us: backward_pass(): pl.pallas_call(functools.partial(backward_kernel, seqs, planes), out_shap...]
    all_gather x3 -> x0, waiting for transfers between devices: 312 us -> none  [the longest x1 278 us: local(): lax.all_gather(master.astype(jnp.bfloat16), ('seq', 'grp'), axis=0, tiled...]
    dot_general x92 -> x0, matrix products: 200 us -> none  [the longest x10 38.8 us: product_tn(): jnp.einsum('rd,re->de', left, right, preferred_element_type=jnp.float32)]
    ppermute x32 -> x0, starting transfers between devices: 130 us -> none  [the longest x16 74 us: passed_along(): return lax.ppermute(block, axis, route)]
    select_n x4 -> x0, other arithmetic: 89.2 us -> none  [the longest x1 66.4 us: local(): jnp.where(occupied[:, None, None], jnp.take(grad_units, unit_at, axis=0),...]
    gather x2 -> x0, local copies, waits for them, and re-layouts: 88.4 us -> none  [the longest x1 65.6 us: local(): jnp.take(grad_units, unit_at, axis=0)]
    unnamed x7 -> x0, waiting for transfers between devices: 68.9 us -> none
  transfers between devices with their start and end apart: 38 -> 0, of which waited for: 5 -> 0; matrix products, arithmetic and copies ran while one was open for 14% -> 0% of each run, Pallas kernels for 0% -> 0%
where the time goes in v1:
time: 471 us; the launch traced here: 470 us
  Pallas kernels  452 us (96%)
  other arithmetic  9.3 us (2%)
  local copies, waits for them, and re-layouts  6.28 us (1%)
    pallas_call x1, Pallas kernels, backward_pass(): pl.pallas_call(functools.partial(backward_kernel, seqs, planes), out_shap...  241 us
    pallas_call x1, Pallas kernels, forward_pass(): pl.pallas_call(functools.partial(forward_kernel, seqs, planes), out_shape...  209 us

profile of v1, /device:TPU:0, one launch (start us, length us, event | category | flops | bytes accessed | tf_op | source)
XLA Modules:
  0.0 469.6 jit_solution(14399916249781090192)
XLA Ops:
  1.9 1.9 owner_tables.1
  3.9 1.5 pad.4.memory_ref
  5.4 209.3 %forward_pass.1 = (bf16[16,2,8,4,4,32,128]{6,5,4,3,2,1,0:T(8,128)(2,1)}, bf16[256,1024]{1,0:T(8,128)(2,1)}, bf16[256,1024]{1,0:T(8,128)(2,1)}, bf16[3,8,256,128]...) custom-call(s32[1]{0:T(128)S(6)} %copy.25.window_ref, ...), custom_call_target="tpu_custom_call" | custom-call | tf_op jit(solution)/shard_map/forward_pass/pallas_call | solution.py:849
  214.7 0.0 copy-start.2
  214.7 0.0 copy-start.4
  214.7 0.0 copy-start.5
  214.7 0.0 copy-start
  214.7 240.8 %backward_pass.1 = (bf16[16,2,4,4,4,32,128]{6,5,4,3,2,1,0:T(8,128)(2,1)}, bf16[16,2,2,4,4,32,128]{6,5,4,3,2,1,0:T(8,128)(2,1)}, bf16[16,2,3,2,2,4,32,128]{7,6,5,...) custom-call(s32[1]{0:T(128)S(6)} %copy.25.window_ref, ...), custom_call_target="tpu_custom_call" | custom-call | tf_op jit(solution)/shard_map/backward_pass/pallas_call | solution.py:1858
  455.5 1.4 slice.12
  456.9 1.6 slice_bitcast_fusion
  458.5 0.0 copy-done.2
  458.5 0.0 copy-done.4
  458.5 0.0 copy-done.5
  458.5 1.7 multiply_subtract_fusion.1
  460.1 0.0 copy-done
  460.1 0.0 copy-start.3
  460.1 0.0 copy-start.1
  460.1 7.6 %fusion.4 = (bf16[3,256,1024]{2,1,0:T(8,128)(2,1)}, f32[3,256,1024]{2,1,0:T(8,128)}, f32[3,256,1024]{2,1,0:T(8,128)}, f32[3,256,1024]{2,1,0:T(8,128)}) fusion(f32[3,256,1024]{2,1,0:T(8,128)S(1)} %copy-done, f32[3,256,1024]{2,1,0:T(8,128)} %param.19, bf16[3,256,1024]{2,1,0:T(8,128)(2,1)} %get-tuple-element.59, f32[3,256,1024]{2,1,0:T(8,128)} %param.20), kind=kLoop, calls=%fused_computation.11 | loop fusion | flops 12582912 | bytes 22020096 | tf_op jit(solution)/shard_map/convert_element_type | solution.py:2775
  467.8 0.0 copy-done.3
  467.8 0.8 copy.27
  468.6 0.0 copy-done.1
  468.6 1.0 copy.28
Async XLA Ops:
  214.7 243.8 %copy-start.2 = (f32[17,1024]{1,0:T(8,128)S(1)}, f32[17,1024]{1,0:T(8,128)}, u32[]{:S(2)}) copy-start(f32[17,1024]{1,0:T(8,128)} %vectors_ref.3) | copy-start | bytes 208900
  214.7 243.8 %copy-start.4 = (f32[17,1024]{1,0:T(8,128)S(1)}, f32[17,1024]{1,0:T(8,128)}, u32[]{:S(2)}) copy-start(f32[17,1024]{1,0:T(8,128)} %param.22) | copy-start | bytes 208900
  214.7 243.8 %copy-start.5 = (f32[17,1024]{1,0:T(8,128)S(1)}, f32[17,1024]{1,0:T(8,128)}, u32[]{:S(2)}) copy-start(f32[17,1024]{1,0:T(8,128)} %param.23) | copy-start | bytes 208900
  214.7 245.4 %copy-start = (f32[3,256,1024]{2,1,0:T(8,128)S(1)}, f32[3,256,1024]{2,1,0:T(8,128)}, u32[]{:S(2)}) copy-start(f32[3,256,1024]{2,1,0:T(8,128)} %master_ref.1) | copy-start | bytes 9437188
  460.1 7.6 %copy-start.3 = (bf16[256,1024]{1,0:T(8,128)(2,1)S(1)}, bf16[256,1024]{1,0:T(8,128)(2,1)}, u32[]{:S(2)}) copy-start(bf16[256,1024]{1,0:T(8,128)(2,1)} %get-tuple-element.38) | copy-start | bytes 1572868
  460.1 8.4 %copy-start.1 = (f32[256,1024]{1,0:T(8,128)S(1)}, f32[256,1024]{1,0:T(8,128)}, u32[]{:S(2)}) copy-start(f32[256,1024]{1,0:T(8,128)} %get-tuple-element.57) | copy-start | bytes 3145732

commit v2 on v1

--- a/solution.py
+++ b/solution.py
@@ -472,6 +472,7 @@
     act_ref,
     slope_ref,
     mixed_ref,
+    padded_ref,
     master_wide,
     master_low,
     tiles,
@@ -529,10 +530,15 @@
 
     def memory_copy(peer, slot):
         return remote(
-            memory_ref, memory_came.at[slot], memory_send.at[peer], memory_recv.at[slot], (peer, z)
+            padded_ref, memory_came.at[slot], memory_send.at[peer], memory_recv.at[slot], (peer, z)
         )
 
     def spread():
+        own_memory = memory_ref[...].astype(F32)
+        if padded_ref.shape[0] > mem_rows:
+            fill = jnp.zeros((padded_ref.shape[0] - mem_rows, D), F32)
+            own_memory = jnp.concatenate([own_memory, fill], 0)
+        padded_ref[...] = own_memory.astype(BF16)
         fetch.wait()
         part = 64
 
@@ -557,7 +563,7 @@
             tiles[here, half] = master_low[:, tile_rows, tile_columns]
 
         loop(0, 2, keep_own)
-        memory_came[me] = memory_ref[...]
+        memory_came[me] = padded_ref[...]
         norm_into(tokens_ref, vector(0), vector(1), h1_ref)
 
         def finish_memory(step):
@@ -813,8 +819,10 @@
 
 
 def forward_pass(
-    seqs, planes, windows, lengths, holder, slot, master, tokens, memory, mem, vectors
+    seqs, planes, windows, lengths, holder, slot, master, tokens, memory, vectors
 ):
+    mem = seqs * memory.shape[0]
+    padded = memory.shape[0] + -memory.shape[0] % 16
     groups = holder.shape[0] // GROUP_UNITS
     slots, unit_rows = master.shape[:2]
     block = (unit_rows // 2 // planes, LANES)
@@ -845,6 +853,7 @@
         shape((rows, FF), BF16),
         shape((rows, FF), BF16),
         shape((rows, D), BF16),
+        shape((padded, D), BF16),
     )
     return pl.pallas_call(
         functools.partial(forward_kernel, seqs, planes),
@@ -856,7 +865,7 @@
             pltpu.VMEM(master.shape, BF16),
             pltpu.VMEM((seqs * planes, 2, slots) + block, BF16),
             pltpu.VMEM((groups, 2, GROUP_UNITS) + block, BF16),
-            pltpu.VMEM((seqs,) + memory.shape, BF16),
+            pltpu.VMEM((seqs, padded, D), BF16),
             pltpu.VMEM((mem, D), F32),
             pltpu.VMEM((mem, D), BF16),
             pltpu.VMEM((4,) + matrix, BF16),
@@ -874,7 +883,9 @@
         ]
         + [dma((3, seqs)), dma((3, seqs)), dma((seqs,)), dma((seqs,))],
         compiler_params=pltpu.CompilerParams(
-            collective_id=2, has_side_effects=True, vmem_limit_bytes=56 * MIB
+            collective_id=2,
+            has_side_effects=True,
+            vmem_limit_bytes=56 * MIB,
         ),
         name="forward_pass",
     )(windows, lengths, holder, slot, master, tokens, memory, vectors)
@@ -1932,7 +1943,9 @@
             dma((2,)),
         ],
         compiler_params=pltpu.CompilerParams(
-            collective_id=3, has_side_effects=True, vmem_limit_bytes=60 * MIB
+            collective_id=3,
+            has_side_effects=True,
+            vmem_limit_bytes=60 * MIB,
         ),
         name="backward_pass",
     )(windows, lengths, group, unit, whole, slope, *arrays)
@@ -2510,7 +2523,6 @@
     mem_rows = memory.shape[1]
     seqs, planes = lax.axis_size("seq"), lax.axis_size("grp")
     holder, slot, group, unit = owner_tables(owners, master.shape[0], seqs * planes)
-    memory_padded = jnp.pad(memory.reshape(mem_rows, D), ((0, -mem_rows % 16), (0, 0)))
     flat = tokens.reshape(rows, D)
     (
         whole,
@@ -2530,6 +2542,7 @@
         activation,
         slope,
         mixed,
+        memory_padded,
     ) = forward_pass(
         seqs,
         planes,
@@ -2539,8 +2552,7 @@
         slot,
         master,
         flat,
-        memory_padded,
-        seqs * mem_rows,
+        memory.reshape(mem_rows, D),
         vectors,
     )
     grad_slots, grad_tokens, grad_memory, vector_sums = backward_pass(
@@ -2573,13 +2585,7 @@
             vectors,
         ),
     )
-    return (
-        mixed.reshape(tokens.shape),
-        grad_tokens.reshape(tokens.shape),
-        grad_memory[:mem_rows].reshape(memory.shape),
-        grad_slots,
-        vector_sums[: vectors.shape[0]],
-    )
+    return mixed.reshape(tokens.shape), grad_tokens.reshape(tokens.shape), grad_memory, grad_slots, vector_sums
 
 
 def plain_layer(
@@ -2749,6 +2755,74 @@
     return mixed, grad_tokens, grad_memory, grad_slots, grad_vectors
 
 
+def update_kernel(
+    master_ref,
+    first_ref,
+    second_ref,
+    grad_ref,
+    vectors_ref,
+    vec_first_ref,
+    vec_second_ref,
+    vec_grad_ref,
+    memory_ref,
+    first_out,
+    second_out,
+    master_out,
+    low_out,
+    vec_first_out,
+    vec_second_out,
+    vectors_out,
+    memory_out,
+    bias_out,
+):
+    first, second, weight = adam_step(
+        master_ref[...],
+        first_ref[...],
+        second_ref[...],
+        grad_ref[...].astype(F32),
+        RATE_MATRIX,
+        WEIGHT_DECAY,
+    )
+    first_out[...] = first
+    second_out[...] = second
+    master_out[...] = weight
+    low_out[...] = weight.astype(BF16)
+
+    @pl.when((pl.program_id(0) == 0) & (pl.program_id(1) == 0))
+    def _():
+        rows = vectors_ref.shape[0]
+        sums = vec_grad_ref[...][:rows]
+        vec_first_out[...], vec_second_out[...], vectors_out[...] = adam_step(
+            vectors_ref[...], vec_first_ref[...], vec_second_ref[...], sums, RATE_VECTOR, 0.0
+        )
+        memory_out[...] = memory_ref[...][: memory_out.shape[0]]
+        bias_out[...] = sums[rows - 1 :]
+
+
+def update(master, first, second, grad, vectors, vec_first, vec_second, vec_grad, grad_memory, mem):
+    slots, rows, width = master.shape
+    part = rows // 2
+    block = pl.BlockSpec((1, part, width), lambda s, p: (s, p, 0))
+
+    def whole(shape):
+        return pl.BlockSpec(shape, lambda s, p: (0, 0))
+
+    shape = jax.ShapeDtypeStruct
+    vec = whole(vectors.shape)
+    return pl.pallas_call(
+        update_kernel,
+        grid=(slots, rows // part),
+        out_shape=(shape(master.shape, F32),) * 3
+        + (shape(master.shape, BF16),)
+        + (shape(vectors.shape, F32),) * 3
+        + (shape((mem, width), F32), shape((1, width), F32)),
+        in_specs=[block] * 4 + [vec] * 3 + [whole(vec_grad.shape), whole(grad_memory.shape)],
+        out_specs=(block,) * 4 + (vec,) * 3 + (whole((mem, width)), whole((1, width))),
+        compiler_params=pltpu.CompilerParams(vmem_limit_bytes=60 * MIB),
+        name="update",
+    )(master, first, second, grad, vectors, vec_first, vec_second, vec_grad, grad_memory)
+
+
 def local(
     tokens,
     memory,
@@ -2768,15 +2842,45 @@
     mixed, grad_tokens, grad_memory, grad_slots, grad_vectors = layer(
         tokens, memory, cotangent, windows, mem_lengths, owners, master, vectors
     )
-    grad_slots = grad_slots.astype(F32)
-    new_first, new_second, new_master = adam_step(
-        master, first_moment, second_moment, grad_slots, RATE_MATRIX, WEIGHT_DECAY
-    )
-    master_copy = new_master.astype(BF16)
-    vec_first_out, vec_second_out, vectors_out = adam_step(
-        vectors, vec_first, vec_second, grad_vectors, RATE_VECTOR, 0.0
-    )
-    grad_out_bias = grad_vectors[vectors.shape[0] - 1]
+    if tiled:
+        (
+            new_first,
+            new_second,
+            new_master,
+            master_copy,
+            vec_first_out,
+            vec_second_out,
+            vectors_out,
+            grad_memory,
+            grad_out_bias,
+        ) = update(
+            master,
+            first_moment,
+            second_moment,
+            grad_slots,
+            vectors,
+            vec_first,
+            vec_second,
+            grad_vectors,
+            grad_memory,
+            memory.shape[1],
+        )
+        grad_memory = grad_memory.reshape(memory.shape)
+        grad_out_bias = grad_out_bias.reshape(D)
+    else:
+        new_first, new_second, new_master = adam_step(
+            master,
+            first_moment,
+            second_moment,
+            grad_slots.astype(F32),
+            RATE_MATRIX,
+            WEIGHT_DECAY,
+        )
+        master_copy = new_master.astype(BF16)
+        vec_first_out, vec_second_out, vectors_out = adam_step(
+            vectors, vec_first, vec_second, grad_vectors, RATE_VECTOR, 0.0
+        )
+        grad_out_bias = grad_vectors[vectors.shape[0] - 1]
     return (
         mixed,
         grad_tokens,

time: 471 us -> 468 us (level)
  Pallas kernels: 452 us -> 463 us
  other arithmetic: 9.3 us -> 0 us
    pallas_call x0 -> x1, Pallas kernels: none -> 11.2 us  [update(): pl.pallas_call(update_kernel, grid=(slots, rows // part), out_shape=(shap...]
    convert_element_type x1 -> x0, other arithmetic: 7.64 us -> none  [local(): master_copy = new_master.astype(BF16)]
where the time goes in v2:
time: 468 us; the launch traced here: 467 us
  Pallas kernels  463 us (99%)
    pallas_call x1, Pallas kernels, backward_pass(): pl.pallas_call(functools.partial(backward_kernel, seqs, planes), out_shap...  240 us
    pallas_call x1, Pallas kernels, forward_pass(): pl.pallas_call(functools.partial(forward_kernel, seqs, planes), out_shape...  209 us
    pallas_call x1, Pallas kernels, update(): pl.pallas_call(update_kernel, grid=(slots, rows // part), out_shape=(shap...  11.2 us

profile of v2, /device:TPU:0, one launch (start us, length us, event | category | flops | bytes accessed | tf_op | source)
XLA Modules:
  0.0 466.7 jit_solution(6087821892369993382)
XLA Ops:
  1.9 1.9 owner_tables.1
  3.9 209.4 %forward_pass.1 = (bf16[16,2,8,4,4,32,128]{6,5,4,3,2,1,0:T(8,128)(2,1)}, bf16[256,1024]{1,0:T(8,128)(2,1)}, bf16[256,1024]{1,0:T(8,128)(2,1)}, bf16[3,8,256,128]...) custom-call(s32[1]{0:T(128)S(6)} %copy.25.window_ref, ...), custom_call_target="tpu_custom_call" | custom-call | tf_op jit(solution)/shard_map/forward_pass/pallas_call | solution.py:858
  213.2 240.4 %backward_pass.1 = (bf16[16,2,4,4,4,32,128]{6,5,4,3,2,1,0:T(8,128)(2,1)}, bf16[16,2,2,4,4,32,128]{6,5,4,3,2,1,0:T(8,128)(2,1)}, bf16[16,2,3,2,2,4,32,128]{7,6,5,...) custom-call(s32[1]{0:T(128)S(6)} %copy.25.window_ref, ...), custom_call_target="tpu_custom_call" | custom-call | tf_op jit(solution)/shard_map/backward_pass/pallas_call | solution.py:1869
  453.7 0.0 copy-start.1
  453.7 0.0 copy-start
  453.7 11.2 %update.1 = (f32[3,256,1024]{2,1,0:T(8,128)}, f32[3,256,1024]{2,1,0:T(8,128)}, f32[3,256,1024]{2,1,0:T(8,128)}, bf16[3,256,1024]{2,1,0:T(8,128)(2,1)}, f32[17,10...) custom-call(f32[3,256,1024]{2,1,0:T(8,128)} %master_ref.3, ...), custom_call_target="tpu_custom_call" | custom-call | tf_op jit(solution)/shard_map/update/pallas_call | solution.py:2812
  464.9 0.0 copy-done.1
  465.0 0.8 copy.27
  465.7 0.0 copy-done
  465.8 1.0 copy.28
Async XLA Ops:
  453.7 11.3 %copy-start.1 = (bf16[256,1024]{1,0:T(8,128)(2,1)S(1)}, bf16[256,1024]{1,0:T(8,128)(2,1)}, u32[]{:S(2)}) copy-start(bf16[256,1024]{1,0:T(8,128)(2,1)} %get-tuple-element.48) | copy-start | bytes 1572868
  453.7 12.1 %copy-start = (f32[256,1024]{1,0:T(8,128)S(1)}, f32[256,1024]{1,0:T(8,128)}, u32[]{:S(2)}) copy-start(f32[256,1024]{1,0:T(8,128)} %get-tuple-element.68) | copy-start | bytes 3145732

commit v3 on v2

--- a/solution.py
+++ b/solution.py
@@ -1814,7 +1814,7 @@
                 work()
 
         for j in range(ups):
-            at(1 + j // 2, functools.partial(hidden_back, j))
+            at(1 + (j + 1) // 2, functools.partial(hidden_back, j))
         at(3, cross_branch)
         blocks = D // LANES
         at(4, functools.partial(cross_back, 0, blocks // 2))
@@ -2801,7 +2801,7 @@
 
 def update(master, first, second, grad, vectors, vec_first, vec_second, vec_grad, grad_memory, mem):
     slots, rows, width = master.shape
-    part = rows // 2
+    part = rows // 4
     block = pl.BlockSpec((1, part, width), lambda s, p: (s, p, 0))
 
     def whole(shape):

time: 468 us -> 470 us (level)
  no operation moved by 1% of the time
where the time goes in v3:
time: 470 us; the launch traced here: 469 us
  Pallas kernels  466 us (99%)
    pallas_call x1, Pallas kernels, backward_pass(): pl.pallas_call(functools.partial(backward_kernel, seqs, planes), out_shap...  240 us
    pallas_call x1, Pallas kernels, forward_pass(): pl.pallas_call(functools.partial(forward_kernel, seqs, planes), out_shape...  209 us
    pallas_call x1, Pallas kernels, update(): pl.pallas_call(update_kernel, grid=(slots, rows // part), out_shape=(shap...  13.8 us

profile of v3, /device:TPU:0, one launch (start us, length us, event | category | flops | bytes accessed | tf_op | source)
XLA Modules:
  0.0 469.3 jit_solution(17915181817136726012)
XLA Ops:
  1.9 1.9 owner_tables.1
  3.9 209.4 %forward_pass.1 = (bf16[16,2,8,4,4,32,128]{6,5,4,3,2,1,0:T(8,128)(2,1)}, bf16[256,1024]{1,0:T(8,128)(2,1)}, bf16[256,1024]{1,0:T(8,128)(2,1)}, bf16[3,8,256,128]...) custom-call(s32[1]{0:T(128)S(6)} %copy.25.window_ref, ...), custom_call_target="tpu_custom_call" | custom-call | tf_op jit(solution)/shard_map/forward_pass/pallas_call | solution.py:858
  213.2 240.4 %backward_pass.1 = (bf16[16,2,4,4,4,32,128]{6,5,4,3,2,1,0:T(8,128)(2,1)}, bf16[16,2,2,4,4,32,128]{6,5,4,3,2,1,0:T(8,128)(2,1)}, bf16[16,2,3,2,2,4,32,128]{7,6,5,...) custom-call(s32[1]{0:T(128)S(6)} %copy.25.window_ref, ...), custom_call_target="tpu_custom_call" | custom-call | tf_op jit(solution)/shard_map/backward_pass/pallas_call | solution.py:1869
  453.6 0.0 copy-start.1
  453.6 0.0 copy-start
  453.6 13.8 %update.1 = (f32[3,256,1024]{2,1,0:T(8,128)}, f32[3,256,1024]{2,1,0:T(8,128)}, f32[3,256,1024]{2,1,0:T(8,128)}, bf16[3,256,1024]{2,1,0:T(8,128)(2,1)}, f32[17,10...) custom-call(f32[3,256,1024]{2,1,0:T(8,128)} %master_ref.3, ...), custom_call_target="tpu_custom_call" | custom-call | tf_op jit(solution)/shard_map/update/pallas_call | solution.py:2812
  467.5 0.0 copy-done.1
  467.5 0.8 copy.27
  468.3 0.0 copy-done
  468.3 1.0 copy.28
Async XLA Ops:
  453.6 13.9 %copy-start.1 = (bf16[256,1024]{1,0:T(8,128)(2,1)S(1)}, bf16[256,1024]{1,0:T(8,128)(2,1)}, u32[]{:S(2)}) copy-start(bf16[256,1024]{1,0:T(8,128)(2,1)} %get-tuple-element.48) | copy-start | bytes 1572868
  453.6 14.7 %copy-start = (f32[256,1024]{1,0:T(8,128)S(1)}, f32[256,1024]{1,0:T(8,128)}, u32[]{:S(2)}) copy-start(f32[256,1024]{1,0:T(8,128)} %get-tuple-element.68) | copy-start | bytes 3145732
